TPU v7x, 768 devices: a whole 4x8x12 slice. The times are simulated.
768 devices in a mesh: dp: 256 (over y, z_hi, x, core), space: 3 (over z_lo).
Axes of the slice: x: 4, y: 8, z: 12 (z_hi: 4, z_lo: 3; z = z_hi * 3 + z_lo), core: 2. Of those that a mesh axis runs over, the one named last changes fastest.
Arguments:
- images: bfloat16 [256, 24, 288, 256], P('dp', 'space'), may hold values from -12 to 12
- w_reduce: bfloat16 [256, 64], replicated, may hold values from -0.375 to 0.375
- w_dilated: bfloat16 [3, 3, 64, 64], replicated, may hold values from -0.25 to 0.25
- w_expand: bfloat16 [64, 256], replicated, may hold values from -0.75 to 0.75
- gain_one: float32 [64], replicated, may hold values from 0.25 to 1.75
- shift_one: float32 [64], replicated, may hold values from -3 to 3
- gain_two: float32 [64], replicated, may hold values from 0.25 to 1.75
- shift_two: float32 [64], replicated, may hold values from -3 to 3
- gain_three: float32 [256], replicated, may hold values from 0.25 to 1.75
- shift_three: float32 [256], replicated, may hold values from -3 to 3
- cotangent: bfloat16 [256, 24, 288, 256], P('dp', 'space'), may hold values from -6 to 6
Outputs:
- result: bfloat16 [256, 24, 288, 256], P('dp', 'space')
- grad_images: bfloat16 [256, 24, 288, 256], P('dp', 'space')
- grad_reduce: float32 [256, 64], replicated
- grad_dilated: float32 [3, 3, 64, 64], replicated
- grad_expand: float32 [64, 256], replicated
- grad_gain_one: float32 [64], replicated
- grad_shift_one: float32 [64], replicated
- grad_gain_two: float32 [64], replicated
- grad_shift_two: float32 [64], replicated
- grad_gain_three: float32 [256], replicated
- grad_shift_three: float32 [256], replicated
All inputs are finite; a program needn't handle non-finite values.
Results may differ from a plain program's by a relative error of at most 0.012.
Values may be sent and summed in bfloat16 or wider, within the bound.
A program may use at most 32 MiB of HBM per device.

v0:
```python
import jax
import jax.numpy as jnp
from jax import lax
from jax.sharding import PartitionSpec as P

epsilon = 1e-05


def extended(block, sides, width):
    for axis, dim in sides:
        count = lax.axis_size(axis)
        forward = [(i, i + 1) for i in range(count - 1)]
        backward = [(target, source) for source, target in forward]
        low = lax.ppermute(
            lax.slice_in_dim(block, block.shape[dim] - width, None, axis=dim), axis, forward
        )
        high = lax.ppermute(lax.slice_in_dim(block, 0, width, axis=dim), axis, backward)
        block = jnp.concatenate([low, block, high], axis=dim)
    return block


def smooth_act(value):
    return value * jax.nn.sigmoid(value)


def smooth_slope(value):
    sig = jax.nn.sigmoid(value)
    return sig * (1.0 + value * (1.0 - sig))


def normalize(pre, gain, shift, count):
    average = lax.psum(jnp.sum(pre, 0), "space") / count
    centred = pre - average
    variance = lax.psum(jnp.sum(centred * centred, 0), "space") / count
    inv_std = lax.rsqrt(variance + epsilon)
    normed = centred * inv_std
    return (normed, inv_std, gain * normed + shift)


def backnorm(grad, normed, inv_std, gain, count):
    local_sum = jnp.sum(grad, 0)
    local_cross = jnp.sum(grad * normed, 0)
    grad_sum, grad_cross = lax.psum((local_sum, local_cross), "space")
    back = (gain * inv_std * (grad - grad_sum / count - normed * grad_cross / count)).astype(
        jnp.bfloat16
    )
    return (back, local_cross, local_sum)


def dilated(padded, kernel, rows, cols):
    output = jnp.zeros((rows * cols, kernel.shape[3]), jnp.float32)
    for tap_row in range(3):
        for tap_col in range(3):
            window = padded[
                2 * tap_row : 2 * tap_row + rows, 2 * tap_col : 2 * tap_col + cols
            ].reshape(rows * cols, -1)
            output = output + jnp.dot(
                window, kernel[tap_row, tap_col], preferred_element_type=jnp.float32
            )
    return output


def contract(left, right):
    return lax.dot_general(
        left, right, (((0,), (0,)), ((), ())), preferred_element_type=jnp.float32
    )


def shards(
    images,
    w_reduce,
    w_dilated,
    w_expand,
    gain_one,
    shift_one,
    gain_two,
    shift_two,
    gain_three,
    shift_three,
    cotangent,
):
    rows, cols, chans = (images.shape[1], images.shape[2], images.shape[3])
    mids = w_reduce.shape[1]
    pixels = rows * cols
    count = float(pixels * lax.axis_size("space"))
    flat_in = images.reshape(pixels, chans)
    pre_one = jnp.dot(flat_in, w_reduce, preferred_element_type=jnp.float32)
    normed_one, istd_one, out_one = normalize(pre_one, gain_one, shift_one, count)
    act_one = smooth_act(out_one).astype(jnp.bfloat16)
    edged_one = extended(act_one.reshape(rows, cols, mids), (("space", 0),), 2)
    padded_one = jnp.pad(edged_one, ((0, 0), (2, 2), (0, 0)))
    pre_two = dilated(padded_one, w_dilated, rows, cols)
    normed_two, istd_two, out_two = normalize(pre_two, gain_two, shift_two, count)
    act_two = smooth_act(out_two).astype(jnp.bfloat16)
    pre_three = jnp.dot(act_two, w_expand, preferred_element_type=jnp.float32)
    normed_three, istd_three, out_three = normalize(pre_three, gain_three, shift_three, count)
    summed = out_three + flat_in.astype(jnp.float32)
    result = smooth_act(summed).astype(jnp.bfloat16)
    grad_three = cotangent.reshape(pixels, chans).astype(jnp.float32) * smooth_slope(summed)
    dh_three, gg_three, gs_three = backnorm(grad_three, normed_three, istd_three, gain_three, count)
    gw_expand = contract(act_two, dh_three)
    back_two = lax.dot_general(
        dh_three, w_expand, (((1,), (1,)), ((), ())), preferred_element_type=jnp.float32
    )
    grad_two = back_two * smooth_slope(out_two)
    dh_two, gg_two, gs_two = backnorm(grad_two, normed_two, istd_two, gain_two, count)
    taps = []
    for tap_row in range(3):
        for tap_col in range(3):
            window = padded_one[
                2 * tap_row : 2 * tap_row + rows, 2 * tap_col : 2 * tap_col + cols
            ].reshape(pixels, mids)
            taps.append(contract(window, dh_two))
    gw_dilated = jnp.stack(taps).reshape(3, 3, mids, mids)
    edged_back = extended(dh_two.reshape(rows, cols, mids), (("space", 0),), 2)
    padded_back = jnp.pad(edged_back, ((0, 0), (2, 2), (0, 0)))
    flipped = jnp.transpose(w_dilated[::-1, ::-1], (0, 1, 3, 2))
    grad_one = dilated(padded_back, flipped, rows, cols) * smooth_slope(out_one)
    dh_one, gg_one, gs_one = backnorm(grad_one, normed_one, istd_one, gain_one, count)
    gw_reduce = contract(flat_in, dh_one)
    back_in = lax.dot_general(
        dh_one, w_reduce, (((1,), (1,)), ((), ())), preferred_element_type=jnp.float32
    )
    grad_images = (back_in + grad_three).astype(jnp.bfloat16).reshape(1, rows, cols, chans)
    batch = float(lax.axis_size("dp"))
    summed_parts = lax.psum(
        (gw_reduce, gw_dilated, gw_expand, gg_one, gs_one, gg_two, gs_two, gg_three, gs_three),
        ("dp", "space"),
    )
    grads = [item / batch for item in summed_parts]
    return (
        result.reshape(1, rows, cols, chans),
        grad_images,
        grads[0],
        grads[1],
        grads[2],
        grads[3],
        grads[4],
        grads[5],
        grads[6],
        grads[7],
        grads[8],
    )


def solution(mesh):
    placed = (
        P("dp", "space", None, None),
        P(),
        P(),
        P(),
        P(),
        P(),
        P(),
        P(),
        P(),
        P(),
        P("dp", "space", None, None),
    )
    return jax.shard_map(
        shards,
        mesh=mesh,
        in_specs=placed,
        out_specs=(
            P("dp", "space", None, None),
            P("dp", "space", None, None),
            P(),
            P(),
            P(),
            P(),
            P(),
            P(),
            P(),
            P(),
            P(),
        ),
        check_vma=False,
    )
```

profile of v0, /device:TPU:1, one launch (start us, length us, event | category | flops | bytes accessed | tf_op | source)
XLA Modules:
  0.0 737.0 jit_solution(8857615364992196983)
XLA Ops:
  7.3 1.9 fusion.47
  9.2 7.3 psum.147
  16.8 4.7 psum.148
  22.2 1.3 collective-permute-start.1
  23.7 4.0 collective-permute-start
  31.4 1.7 fusion.44
  33.1 1.3 reshape.136
  34.8 1.4 reshape.134
  36.6 1.4 reshape.131
  41.2 5.7 psum.149
  47.2 4.7 psum.150
  53.7 4.8 psum.151
  58.9 4.9 psum.152
  63.7 5.1 fusion.40
  68.8 4.7 all-reduce.6
  73.5 2.3 multiply_convert_fusion
  76.7 1.5 fusion.42
  78.2 4.8 all-reduce.5
  83.0 1.5 multiply_convert_fusion.3
  86.8 1.3 collective-permute-start.3
  88.1 4.0 collective-permute-start.2
  98.4 1.0 reshape.145
  100.6 1.2 convolution_add_fusion.7
  103.5 2.5 fusion.41
  106.0 136.6 %all-reduce.2 = (f32[64]{0:T(128)S(1)}, f32[64]{0:T(128)S(1)}, f32[64]{0:T(128)S(1)}, f32[64]{0:T(128)S(1)}, f32[256]{0:T(256)S(1)}, /*index=5*/f32[256]{0:T(256)S(1)}) all-reduce(f32[64]{0:T(128)S(1)} %get-tuple-element.14, f32[64]{0:T(128)S(1)} %get-tuple-element.13, ...), channel_id=1, replica_groups=mesh['dp'=256,'space'=3] {'dp','space'}, use_global_device_ids=true, to_apply=%region_27.28 | all-reduce | flops 768 | bytes 6144 | tf_op jit(solution)/shard_map/psum | solution.py:126
  242.6 4.9 all-reduce.4
  247.6 1.5 multiply_convert_fusion.2
  249.1 1.5 fusion
  253.2 472.2 %all-reduce.9.cloned.1.call-done = (f32[256,64]{0,1:T(8,128)}, f32[3,3,64,64]{3,2,1,0:T(8,128)}, f32[64,256]{1,0:T(8,128)}) async-done(((f32[256,64]{0,1:T(8,128)}, f32[3,3,64,64]{3,2,1,0:T(8,128)}, f32[64,256]{1,0:T(8,128)}), (f32[256,64]{0,1:T(8,128)}, f32[3,3,64,64]{3,2,1,0:T(8,128)}, f32[64,256]{1,0:T(8,128)})) %all-reduce.9.cloned.1.call-update) | async-done | bytes 278544 | tf_op jit(solution)/shard_map/psum | solution.py:126
  725.5 1.5 broadcast_multiply_fusion.2
  726.9 1.5 broadcast_multiply_fusion.1
  728.4 1.7 broadcast_multiply_fusion
  (145 shorter events, 25.7 us)
Async XLA Ops:
  7.2 45.9 %copy-start = (bf16[64,256]{1,0:T(8,128)(2,1)S(1)}, bf16[64,256]{1,0:T(8,128)(2,1)}, u32[]{:S(2)}) copy-start(bf16[64,256]{1,0:T(8,128)(2,1)} %param.14) | copy-start | bytes 98308
  7.2 14.3 %copy-start.30 = (f32[64]{0:T(128)S(1)}, f32[64]{0:T(128)}, u32[]{:S(2)}) copy-start(f32[64]{0:T(128)} %param.15) | copy-start | bytes 772
  7.2 14.3 %copy-start.33 = (f32[64]{0:T(128)S(1)}, f32[64]{0:T(128)}, u32[]{:S(2)}) copy-start(f32[64]{0:T(128)} %param.16) | copy-start | bytes 772
  7.2 21.1 %copy-start.24 = (bf16[3,3,64,64]{3,2,1,0:T(8,128)(2,1)S(1)}, bf16[3,3,64,64]{3,2,1,0:T(8,128)(2,1)}, u32[]{:S(2)}) copy-start(bf16[3,3,64,64]{3,2,1,0:T(8,128)(2,1)} %param.13) | copy-start | bytes 221188
  7.2 718.2 %all-reduce.9.cloned.1.call-start = ((), (), s32[]{:S(2)}) async-start(), calls=%async_computation | async-start | bytes 851968 | tf_op jit(solution)/shard_map/psum | solution.py:126
  9.2 20.8 %copy-start.3 = (f32[2304,64]{0,1:T(8,128)}, f32[2304,64]{0,1:T(8,128)S(1)}, u32[]{:S(2)}) copy-start(f32[2304,64]{0,1:T(8,128)S(1)} %get-tuple-element.61) | copy-start | bytes 1769476
  22.2 6.8 collective-permute-start.1
  23.7 5.6 collective-permute-start
  30.0 10.8 %copy-start.7 = (bf16[2304,64]{0,1:T(8,128)(2,1)}, bf16[2304,64]{0,1:T(8,128)(2,1)S(1)}, u32[]{:S(2)}) copy-start(bf16[2304,64]{0,1:T(8,128)(2,1)S(1)} %reshape.137) | copy-start | bytes 884740
  30.4 8.6 %copy-start.15 = (bf16[2304,64]{0,1:T(8,128)(2,1)}, bf16[2304,64]{0,1:T(8,128)(2,1)S(1)}, u32[]{:S(2)}) copy-start(bf16[2304,64]{0,1:T(8,128)(2,1)S(1)} %reshape.132) | copy-start | bytes 884740
  34.5 6.0 copy-start.13
  34.8 5.4 copy-start.17
  36.2 3.3 copy-start.19
  36.6 3.0 copy-start.21
  40.5 11.3 %copy-start.29 = (f32[64]{0:T(128)S(1)}, f32[64]{0:T(128)}, u32[]{:S(2)}) copy-start(f32[64]{0:T(128)} %param.17) | copy-start | bytes 772
  40.5 11.3 %copy-start.32 = (f32[64]{0:T(128)S(1)}, f32[64]{0:T(128)}, u32[]{:S(2)}) copy-start(f32[64]{0:T(128)} %param.18) | copy-start | bytes 772
  53.1 10.7 %copy-start.28 = (f32[256]{0:T(256)S(1)}, f32[256]{0:T(256)}, u32[]{:S(2)}) copy-start(f32[256]{0:T(256)} %param.19) | copy-start | bytes 3076
  53.1 10.7 %copy-start.31 = (f32[256]{0:T(256)S(1)}, f32[256]{0:T(256)}, u32[]{:S(2)}) copy-start(f32[256]{0:T(256)} %param.20) | copy-start | bytes 3076
  73.4 2.3 copy-start.6
  76.7 7.8 %copy-start.12 = (bf16[2304,64]{0,1:T(8,128)(2,1)S(1)}, bf16[2304,64]{0,1:T(8,128)(2,1)}, u32[]{:S(2)}) copy-start(bf16[2304,64]{0,1:T(8,128)(2,1)} %copy-done.11) | copy-start | bytes 884740
  78.2 6.7 copy-start.16
  78.2 6.9 copy-start.22
  78.2 7.1 copy-start.20
  83.0 2.8 copy-start.18
  84.9 7.2 copy-start.10
  86.8 6.2 collective-permute-start.3
  88.1 5.6 collective-permute-start.2
  92.3 3.8 copy-start.26
  98.0 2.3 copy-start.25
  103.5 145.5 %copy-start.1 = (f32[2304,256]{1,0:T(8,128)S(1)}, f32[2304,256]{1,0:T(8,128)}, u32[]{:S(2)}) copy-start(f32[2304,256]{1,0:T(8,128)} %get-tuple-element.32) | copy-start | bytes 7077892
  103.5 145.6 %copy-start.27 = (bf16[256,64]{0,1:T(8,128)(2,1)S(1)}, bf16[256,64]{0,1:T(8,128)(2,1)}, u32[]{:S(2)}) copy-start(bf16[256,64]{0,1:T(8,128)(2,1)} %param.12) | copy-start | bytes 98308
  247.6 3.0 copy-start.2
  (7 other events, 8.9 us)
Sparse Core Ops, SparseCore 0:
  252.8 472.6 all-reduce.8
where the time goes:
time: 738 us; the launch traced here: 737 us
  waiting for transfers between devices  473 us (64%)
  blocking collectives  183 us (25%)
  other arithmetic  21.2 us (3%)
  matrix products  17.3 us (2%)
  local copies, waits for them, and re-layouts  16.6 us (2%)
  between operations  14.9 us (2%)
  starting transfers between devices  10.6 us (1%)
    psum x1, waiting for transfers between devices, shards(): lax.psum((gw_reduce, gw_dilated, gw_expand, gg_one, gs_one, gg_two, gs_tw...  472 us
    psum x1, blocking collectives, shards(): lax.psum((gw_reduce, gw_dilated, gw_expand, gg_one, gs_one, gg_two, gs_tw...  137 us
    psum x3, blocking collectives, normalize(): average = lax.psum(jnp.sum(pre, 0), 'space') / count  17.8 us
  transfers between devices with their start and end apart: 5, of which 3 were waited for; matrix products, arithmetic and copies ran while one was open for 0% of the time, Pallas kernels for 0%

commit v1 on v0

v1 whole, which is shorter than its diff:
```python
import functools

import jax
import jax.numpy as jnp
from jax import lax
from jax.experimental import pallas as pl
from jax.experimental.pallas import tpu as pltpu
from jax.sharding import PartitionSpec as P

MESH = pl.DeviceIdType.MESH
f32 = jnp.float32
bf16 = jnp.bfloat16
epsilon = 1e-05

SPLITS = {256: (8, 8, 4), 4: (2, 2, 1)}
MAIN_ROWS = 512
LATE_ROWS = 128
VEC = 448


def part_sum(x):
    n, lanes = x.shape
    return jnp.sum(x.reshape(n // 8, 8, lanes), axis=0)


def both(v8):
    v8 = v8 + pltpu.roll(v8, 64, 1)
    return jnp.sum(v8, axis=0, keepdims=True)


def total(v8):
    return jnp.sum(v8, axis=0, keepdims=True)


def gates(v):
    half = 0.5 * v
    t = jnp.tanh(half)
    act = half * t + half
    sig = 0.5 * t + 0.5
    slope = sig + act * (0.5 - 0.5 * t)
    return act, slope


def dotf(a, b):
    return jnp.dot(a, b, preferred_element_type=f32)


def dot_t(a, b):
    return lax.dot_general(a, b, (((1,), (1,)), ((), ())), preferred_element_type=f32)


def kernel(
    splits,
    images, wr, wd, we, g1, s1, g2, s2, g3, s3, cot,
    result, gimages, o_reduce, o_dilated, o_expand, o_vec,
    img_v, cot_v, res_v, gi_v,
    w_in, w_out, w_fwd, w_bwd,
    pre1, slope1, pre2, slope2, act2, x3, e3, dh3, grad2, grad1, dh1,
    edge1, edge2, halo1, halo2, wide1, wide2,
    xbuf,
    main_a, main_ra, main_b, main_rb, main_c, main_gb, main_ga,
    late_a, late_ra, late_b, late_c, late_ga,
    in_sem, out_sem, hs_sem, hr_sem, xs_sem, xr_sem, send_sem, recv_sem,
):
    ends, ys, highs = splits
    spaces = lax.axis_size("space")
    zs = highs * spaces
    d = lax.axis_index("dp")
    s = lax.axis_index("space")
    end = lax.rem(d, ends)
    high = lax.rem(lax.div(d, ends), highs)
    y = lax.div(d, ends * highs)
    z = high * spaces + s
    cols = 288
    local = 2304.0
    count = local * spaces

    def id_a(k):
        return (d - end + k, s)

    def id_b(k):
        return (d + (k - y) * (ends * highs), s)

    def id_c(k):
        kh = lax.div(k, spaces)
        return (d + (kh - high) * ends, lax.rem(k, spaces))

    groups = {"a": (ends, end, id_a), "b": (ys, y, id_b), "c": (zs, z, id_c)}

    in_copies = []
    for r in range(8):
        c = pltpu.make_async_copy(images.at[0, r], img_v.at[r % 2, r // 2], in_sem.at[r])
        c.start()
        in_copies.append(c)
    cot_copy = pltpu.make_async_copy(cot.at[0], cot_v, in_sem.at[8])
    cot_copy.start()

    barrier = pltpu.get_barrier_semaphore()
    partners = 0
    for name in "abc":
        n, me, ident = groups[name]
        for k in range(1, n):
            pl.semaphore_signal(
                barrier, inc=1, device_id=ident(lax.rem(me + k, n)), device_id_type=MESH
            )
            partners += 1

    zero_in = jnp.zeros((256, 64), bf16)
    w_in[0] = jnp.concatenate([wr[...], zero_in], axis=1)
    w_in[1] = jnp.concatenate([zero_in, wr[...]], axis=1)
    zero_out = jnp.zeros((64, 256), bf16)
    w_out[0] = jnp.concatenate([we[...], zero_out], axis=0)
    w_out[1] = jnp.concatenate([zero_out, we[...]], axis=0)
    zero_mid = jnp.zeros((64, 64), bf16)
    for a in range(3):
        for b in range(3):
            w = wd[a, b]
            diag = jnp.concatenate(
                [
                    jnp.concatenate([w, zero_mid], axis=1),
                    jnp.concatenate([zero_mid, w], axis=1),
                ],
                axis=0,
            )
            w_fwd[a, b * 128 : (b + 1) * 128, :] = diag
            w_bwd[2 - a, :, (2 - b) * 128 : (3 - b) * 128] = diag

    @pl.when(s == 0)
    def _():
        wide1[0:cols, :] = jnp.zeros((cols, 384), bf16)
        wide2[0:cols, :] = jnp.zeros((cols, 384), bf16)

    @pl.when(s == spaces - 1)
    def _():
        wide1[5 * cols : 6 * cols, :] = jnp.zeros((cols, 384), bf16)
        wide2[5 * cols : 6 * cols, :] = jnp.zeros((cols, 384), bf16)

    def twice(ref):
        v = ref[...]
        return jnp.concatenate([v, v], axis=1)

    def send_stats(idx, first, second):
        lanes = first.shape[1]
        xbuf[idx, s, 0:1, 0:lanes] = first
        xbuf[idx, s, 1:2, 0:lanes] = second
        for k in range(1, 3):
            pltpu.make_async_remote_copy(
                src_ref=xbuf.at[idx, s],
                dst_ref=xbuf.at[idx, s],
                send_sem=xs_sem.at[idx, k - 1],
                recv_sem=xr_sem.at[idx, s],
                device_id=(d, lax.rem(s + k, spaces)),
                device_id_type=MESH,
            ).start()

    def wait_stats(idx, lanes):
        for k in range(1, 3):
            f = lax.rem(s + k, spaces)
            pltpu.make_async_remote_copy(
                src_ref=xbuf.at[idx, f],
                dst_ref=xbuf.at[idx, f],
                send_sem=xs_sem.at[idx, k - 1],
                recv_sem=xr_sem.at[idx, f],
                device_id=(d, f),
                device_id_type=MESH,
            ).wait_recv()
        firsts = [xbuf[idx, j, 0:1, 0:lanes] for j in range(3)]
        seconds = [xbuf[idx, j, 1:2, 0:lanes] for j in range(3)]
        return firsts, seconds

    def moments(idx, lanes):
        means, squares = wait_stats(idx, lanes)
        mu = (means[0] + means[1] + means[2]) * (1.0 / 3.0)
        spread = sum((m - mu) * (m - mu) for m in means)
        var = (squares[0] + squares[1] + squares[2] + local * spread) * (1.0 / count)
        return mu, lax.rsqrt(var + epsilon)

    def sums(idx, lanes):
        firsts, seconds = wait_stats(idx, lanes)
        return firsts[0] + firsts[1] + firsts[2], seconds[0] + seconds[1] + seconds[2]

    def halo(edge, halos, which):
        @pl.when(s > 0)
        def _():
            pltpu.make_async_remote_copy(
                src_ref=edge.at[0], dst_ref=halos.at[1],
                send_sem=hs_sem.at[which, 0], recv_sem=hr_sem.at[which, 1],
                device_id=(d, s - 1), device_id_type=MESH,
            ).start()

        @pl.when(s < spaces - 1)
        def _():
            pltpu.make_async_remote_copy(
                src_ref=edge.at[1], dst_ref=halos.at[0],
                send_sem=hs_sem.at[which, 1], recv_sem=hr_sem.at[which, 0],
                device_id=(d, s + 1), device_id_type=MESH,
            ).start()

    def widen(wide, pair, x):
        at = pair * cols
        spot = lax.broadcasted_iota(jnp.int32, (cols, 128), 0)
        before = jnp.where(spot >= 2, pltpu.roll(x, 2, 0), 0.0)
        after = jnp.where(spot < cols - 2, pltpu.roll(x, cols - 2, 0), 0.0)
        wide[at : at + cols, 0:128] = before.astype(bf16)
        wide[at : at + cols, 128:256] = x.astype(bf16)
        wide[at : at + cols, 256:384] = after.astype(bf16)

    def take_halo(edge, halos, wide, which):
        @pl.when(s > 0)
        def _():
            pltpu.make_async_remote_copy(
                src_ref=edge.at[1], dst_ref=halos.at[0],
                send_sem=hs_sem.at[which, 0], recv_sem=hr_sem.at[which, 0],
                device_id=(d, s - 1), device_id_type=MESH,
            ).wait_recv()
            widen(wide, 0, halos[0].astype(f32))

        @pl.when(s < spaces - 1)
        def _():
            pltpu.make_async_remote_copy(
                src_ref=edge.at[0], dst_ref=halos.at[1],
                send_sem=hs_sem.at[which, 1], recv_sem=hr_sem.at[which, 1],
                device_id=(d, s + 1), device_id_type=MESH,
            ).wait_recv()
            widen(wide, 5, halos[1].astype(f32))

    def end_halo(edge, halos, which):
        @pl.when(s > 0)
        def _():
            pltpu.make_async_remote_copy(
                src_ref=edge.at[0], dst_ref=halos.at[1],
                send_sem=hs_sem.at[which, 0], recv_sem=hr_sem.at[which, 1],
                device_id=(d, s - 1), device_id_type=MESH,
            ).wait_send()

        @pl.when(s < spaces - 1)
        def _():
            pltpu.make_async_remote_copy(
                src_ref=edge.at[1], dst_ref=halos.at[0],
                send_sem=hs_sem.at[which, 1], recv_sem=hr_sem.at[which, 0],
                device_id=(d, s + 1), device_id_type=MESH,
            ).wait_send()

    def conv_fwd(pair, n):
        acc = dotf(wide1[pair * cols : (pair + n) * cols, :], w_fwd[0])
        for a in range(1, 3):
            acc += dotf(wide1[(pair + a) * cols : (pair + a + n) * cols, :], w_fwd[a])
        return acc

    def conv_bwd(pair, n):
        acc = dot_t(wide2[pair * cols : (pair + n) * cols, :], w_bwd[0])
        for a in range(1, 3):
            acc += dot_t(wide2[(pair + a) * cols : (pair + a + n) * cols, :], w_bwd[a])
        return acc

    def local_moments(idx, pre, acc):
        mean = both(acc) * (1.0 / local)
        sq = jnp.zeros((8, 128), f32)
        for p in range(4):
            c = pre[p] - mean
            sq += part_sum(c * c)
        send_stats(idx, mean, both(sq))

    def copy_to(stage, name, src, dst, k):
        n, me, ident = groups[name]
        t = lax.rem(me + k, n)
        return pltpu.make_async_remote_copy(
            src_ref=src(t), dst_ref=dst(me),
            send_sem=send_sem.at[stage, k], recv_sem=recv_sem.at[stage, me],
            device_id=ident(t), device_id_type=MESH,
        )

    def spread_out(stage, name, src, dst):
        for k in range(1, groups[name][0]):
            copy_to(stage, name, src, dst, k).start()

    def collect(stage, name, src, dst):
        n, me, ident = groups[name]
        for k in range(1, n):
            f = lax.rem(me + k, n)
            pltpu.make_async_remote_copy(
                src_ref=src(f), dst_ref=dst(f),
                send_sem=send_sem.at[stage, k], recv_sem=recv_sem.at[stage, f],
                device_id=ident(f), device_id_type=MESH,
            ).wait_recv()

    def added(ref, n):
        acc = ref[0].astype(f32)
        for k in range(1, n):
            acc += ref[k].astype(f32)
        return acc

    acc = jnp.zeros((8, 128), f32)
    for p in range(4):
        in_copies[2 * p].wait()
        in_copies[2 * p + 1].wait()
        v = dotf(img_v[0, p], w_in[0]) + dotf(img_v[1, p], w_in[1])
        pre1[p] = v
        acc += part_sum(v)
    gain1, shift1 = twice(g1), twice(s1)
    gain2, shift2 = twice(g2), twice(s2)
    pl.semaphore_wait(barrier, partners)
    local_moments(0, pre1, acc)
    mu, istd1 = moments(0, 128)
    for p in (0, 3, 1, 2):
        xhat = (pre1[p] - mu) * istd1
        act, slope = gates(gain1 * xhat + shift1)
        pre1[p] = xhat
        slope1[p] = slope
        if p == 0:
            edge1[0] = act.astype(bf16)
        if p == 3:
            edge1[1] = act.astype(bf16)
            halo(edge1, halo1, 0)
        widen(wide1, p + 1, act)

    v = conv_fwd(1, 2)
    pre2[1] = v[0:cols]
    pre2[2] = v[cols : 2 * cols]
    acc = part_sum(v)
    take_halo(edge1, halo1, wide1, 0)
    for p in (0, 3):
        v = conv_fwd(p, 1)
        pre2[p] = v
        acc += part_sum(v)
    local_moments(1, pre2, acc)
    mu, istd2 = moments(1, 128)
    acc3 = jnp.zeros((8, 256), f32)
    for p in range(4):
        xhat = (pre2[p] - mu) * istd2
        act, slope = gates(gain2 * xhat + shift2)
        pre2[p] = xhat
        slope2[p] = slope
        act = act.astype(bf16)
        act2[p] = act
        for q in range(2):
            v = dotf(act, w_out[q])
            x3[2 * p + q] = v
            acc3 += part_sum(v)

    mean = total(acc3) * (1.0 / local)

    def square(r, acc):
        c = x3[r] - mean
        return acc + part_sum(c * c)

    sq = lax.fori_loop(0, 8, square, jnp.zeros((8, 256), f32))
    send_stats(2, mean, total(sq))
    cot_copy.wait()
    gain3, shift3 = g3[...], s3[...]
    mu, istd3 = moments(2, 256)

    def third(r, carry):
        sd, sx = carry
        p, q = lax.div(r, 2), lax.rem(r, 2)
        xhat = (x3[r] - mu) * istd3
        act, slope = gates(gain3 * xhat + shift3 + img_v[q, p].astype(f32))
        res_v[r] = act.astype(bf16)
        e = cot_v[r].astype(f32) * slope
        x3[r] = xhat
        e3[r] = e
        pltpu.make_async_copy(res_v.at[r], result.at[0, r], out_sem.at[0, r]).start()
        return sd + part_sum(e), sx + part_sum(e * xhat)

    zero8 = jnp.zeros((8, 256), f32)
    sd, sx = lax.fori_loop(0, 8, third, (zero8, zero8))
    sd3, sx3 = total(sd), total(sx)
    send_stats(3, sd3, sx3)
    sd, sx = sums(3, 256)
    k0 = gain3 * istd3
    k1 = k0 * sd * (1.0 / count)
    k2 = k0 * sx * (1.0 / count)
    sd_acc = jnp.zeros((8, 128), f32)
    sx_acc = jnp.zeros((8, 128), f32)
    for p in range(4):
        for q in range(2):
            r = 2 * p + q
            dh3[q, p] = (k0 * e3[r] - k1 - k2 * x3[r]).astype(bf16)
        back = dot_t(dh3[0, p], w_out[0]) + dot_t(dh3[1, p], w_out[1])
        g = back * slope2[p]
        grad2[p] = g
        sd_acc += part_sum(g)
        sx_acc += part_sum(g * pre2[p])
    sd2, sx2 = both(sd_acc), both(sx_acc)
    send_stats(4, sd2, sx2)
    rows = 4 * cols
    act_t = act2[...].reshape(rows, 128).T
    expand = dotf(act_t[0:64], dh3[0].reshape(rows, 256)) + dotf(
        act_t[64:128], dh3[1].reshape(rows, 256)
    )
    sd, sx = sums(4, 128)
    k0 = gain2 * istd2
    k1 = k0 * sd * (1.0 / count)
    k2 = k0 * sx * (1.0 / count)
    pieces = []
    for p in (0, 3, 1, 2):
        dh = k0 * grad2[p] - k1 - k2 * pre2[p]
        if p == 0:
            edge2[0] = dh.astype(bf16)
        if p == 3:
            edge2[1] = dh.astype(bf16)
            halo(edge2, halo2, 1)
        widen(wide2, p + 1, dh)

    sd_acc = jnp.zeros((8, 128), f32)
    sx_acc = jnp.zeros((8, 128), f32)

    def first_back(p, v, sd_acc, sx_acc):
        g = v * slope1[p]
        grad1[p] = g
        return sd_acc + part_sum(g), sx_acc + part_sum(g * pre1[p])

    v = conv_bwd(1, 2)
    sd_acc, sx_acc = first_back(1, v[0:cols], sd_acc, sx_acc)
    sd_acc, sx_acc = first_back(2, v[cols : 2 * cols], sd_acc, sx_acc)
    take_halo(edge2, halo2, wide2, 1)
    for p in (0, 3):
        sd_acc, sx_acc = first_back(p, conv_bwd(p, 1), sd_acc, sx_acc)
    sd1, sx1 = both(sd_acc), both(sx_acc)
    send_stats(5, sd1, sx1)

    main_rows = MAIN_ROWS // ends
    late_rows = LATE_ROWS // ends

    def put_main(row, block):
        n = block.shape[0]
        done = 0
        while done < n:
            piece, off = divmod(row + done, main_rows)
            size = min(n - done, main_rows - off)
            main_a[piece, off : off + size, :] = block[done : done + size].astype(bf16)
            done += size

    dh2_t = wide2[cols : cols + rows, 128:256].T
    low = lax.broadcasted_iota(jnp.int32, (64, 128), 1) < 64
    taps = []
    for a in range(3):
        g = dotf(dh2_t, wide1[a * cols : a * cols + rows, :])
        for b in range(3):
            g0 = g[0:64, b * 128 : (b + 1) * 128]
            g1v = g[64:128, b * 128 : (b + 1) * 128]
            if (3 * a + b) % 2 == 0:
                taps.append(g0 + pltpu.roll(g1v, 64, 1))
            else:
                taps.append(pltpu.roll(g0, 64, 1) + g1v)
    taps.append(jnp.zeros((64, 128), f32))
    for u in range(5):
        put_main(64 * u, jnp.where(low, taps[2 * u], taps[2 * u + 1]))
    put_main(320, expand[:, 0:128])
    put_main(384, expand[:, 128:256])
    low1 = lax.broadcasted_iota(jnp.int32, (1, 128), 1) < 64
    vec = jnp.concatenate(
        [
            sx3[:, 0:128], sx3[:, 128:256], sd3[:, 0:128], sd3[:, 128:256],
            jnp.where(low1, sx2, sd2), jnp.where(low1, sx1, sd1),
            jnp.zeros((2, 128), f32),
        ],
        axis=0,
    )
    vec_high = vec.astype(bf16)
    vec_low = vec - vec_high.astype(f32)
    put_main(VEC, jnp.concatenate([vec_high.astype(f32), vec_low], axis=0))
    put_main(VEC + 16, jnp.zeros((48, 128), f32))
    main_ra[end] = main_a[end]

    a_src, a_dst = (lambda t: main_a.at[t]), (lambda me: main_ra.at[me])
    spread_out(0, "a", a_src, a_dst)

    sd, sx = sums(5, 128)
    k0 = gain1 * istd1
    k1 = k0 * sd * (1.0 / count)
    k2 = k0 * sx * (1.0 / count)
    for p in range(4):
        dh1[p] = (k0 * grad1[p] - k1 - k2 * pre1[p]).astype(bf16)
    dh1_t = dh1[...].reshape(rows, 128).T
    reduce = dotf(dh1_t[0:64], img_v[0].reshape(rows, 256)) + dotf(
        dh1_t[64:128], img_v[1].reshape(rows, 256)
    )
    for h in range(2):
        for piece in range(ends):
            lo, hi = piece * late_rows, (piece + 1) * late_rows
            a, b = max(lo, 64 * h), min(hi, 64 * h + 64)
            if a < b:
                late_a[piece, a - lo : b - lo, :] = reduce[
                    a - 64 * h : b - 64 * h, 128 * h : 128 * h + 128
                ].astype(bf16)
    late_ra[end] = late_a[end]
    la_src, la_dst = (lambda t: late_a.at[t]), (lambda me: late_ra.at[me])
    spread_out(5, "a", la_src, la_dst)

    def last(p, carry):
        dh = dh1[p]
        for q in range(2):
            r = 2 * p + q
            gi_v[r] = (dot_t(dh, w_in[q]) + e3[r]).astype(bf16)
            pltpu.make_async_copy(gi_v.at[r], gimages.at[0, r], out_sem.at[1, r]).start()
        return carry

    collect(0, "a", a_src, a_dst)
    part = added(main_ra, ends)
    sub = main_rows // ys
    for k in range(ys):
        main_b[k] = part[k * sub : (k + 1) * sub]
    main_rb[y] = main_b[y]
    b_src, b_dst = (lambda t: main_b.at[t]), (lambda me: main_rb.at[me])
    spread_out(1, "b", b_src, b_dst)

    lax.fori_loop(0, 2, last, 0)

    collect(5, "a", la_src, la_dst)
    late_b[y] = added(late_ra, ends).astype(bf16)
    lb_src, lb_dst = (lambda t: late_b.at[y]), (lambda me: late_b.at[me])
    spread_out(6, "b", lb_src, lb_dst)

    collect(1, "b", b_src, b_dst)
    main_c[z] = added(main_rb, ys)
    c_src, c_dst = (lambda t: main_c.at[z]), (lambda me: main_c.at[me])
    spread_out(2, "c", c_src, c_dst)

    lax.fori_loop(2, 4, last, 0)

    collect(6, "b", lb_src, lb_dst)
    late_c[z] = added(late_b, ys).astype(bf16)
    lc_src, lc_dst = (lambda t: late_c.at[z]), (lambda me: late_c.at[me])
    spread_out(7, "c", lc_src, lc_dst)

    collect(2, "c", c_src, c_dst)
    main_gb[y] = added(main_c, zs)
    gb_src, gb_dst = (lambda t: main_gb.at[y]), (lambda me: main_gb.at[me])
    spread_out(3, "b", gb_src, gb_dst)

    collect(7, "c", lc_src, lc_dst)
    late_ga[end] = added(late_c, zs).astype(bf16)
    lg_src, lg_dst = (lambda t: late_ga.at[end]), (lambda me: late_ga.at[me])
    spread_out(8, "a", lg_src, lg_dst)

    collect(3, "b", gb_src, gb_dst)
    whole = main_gb[...].reshape(main_rows, 128)
    main_ga[end] = whole.astype(bf16)

    @pl.when(end == VEC // main_rows)
    def _():
        at = VEC % main_rows
        v = whole[at : at + 8] + whole[at + 8 : at + 16]
        v_high = v.astype(bf16).astype(f32)
        main_ga[end, at : at + 16, :] = jnp.concatenate([v_high, v - v_high], axis=0).astype(bf16)

    ga_src, ga_dst = (lambda t: main_ga.at[end]), (lambda me: main_ga.at[me])
    spread_out(4, "a", ga_src, ga_dst)

    scale = 1.0 / lax.axis_size("dp")
    collect(8, "a", lg_src, lg_dst)
    late = late_ga[...].reshape(LATE_ROWS, 128).astype(f32).T * scale
    o_reduce[0:128, :] = late[:, 0:64]
    o_reduce[128:256, :] = late[:, 64:128]

    collect(4, "a", ga_src, ga_dst)
    main = main_ga[...].reshape(MAIN_ROWS, 128).astype(f32) * scale
    for u in range(5):
        pair = main[64 * u : 64 * u + 64]
        pair = jnp.concatenate([pair, pair], axis=0).T
        o_dilated[2 * u] = pair[0:64, 0:64]
        if u < 4:
            o_dilated[2 * u + 1] = pair[64:128, 0:64]
    o_expand[:, 0:128] = main[320:384]
    o_expand[:, 128:256] = main[384:448]
    o_vec[...] = main[VEC : VEC + 8] + main[VEC + 8 : VEC + 16]

    for idx in range(6):
        for k in range(1, 3):
            pltpu.make_async_remote_copy(
                src_ref=xbuf.at[idx, s], dst_ref=xbuf.at[idx, s],
                send_sem=xs_sem.at[idx, k - 1], recv_sem=xr_sem.at[idx, s],
                device_id=(d, lax.rem(s + k, spaces)), device_id_type=MESH,
            ).wait_send()
    end_halo(edge1, halo1, 0)
    end_halo(edge2, halo2, 1)
    for stage, name, src, dst in (
        (0, "a", a_src, a_dst), (1, "b", b_src, b_dst), (2, "c", c_src, c_dst),
        (3, "b", gb_src, gb_dst), (4, "a", ga_src, ga_dst), (5, "a", la_src, la_dst),
        (6, "b", lb_src, lb_dst), (7, "c", lc_src, lc_dst), (8, "a", lg_src, lg_dst),
    ):
        for k in range(1, groups[name][0]):
            copy_to(stage, name, src, dst, k).wait_send()
    for r in range(8):
        pltpu.make_async_copy(res_v.at[r], result.at[0, r], out_sem.at[0, r]).wait()
        pltpu.make_async_copy(gi_v.at[r], gimages.at[0, r], out_sem.at[1, r]).wait()


def solution(mesh):
    splits = SPLITS[mesh.shape["dp"]]
    ends, ys, highs = splits
    zs = highs * mesh.shape["space"]
    main_rows = MAIN_ROWS // ends
    late_rows = LATE_ROWS // ends
    sub = main_rows // ys

    def shards(images, wr, wd, we, g1, s1, g2, s2, g3, s3, cot):
        vmem = pl.BlockSpec(memory_space=pltpu.VMEM)
        hbm = pl.BlockSpec(memory_space=pl.ANY)
        big = jax.ShapeDtypeStruct(images.shape, bf16)
        maps = lambda: pltpu.VMEM((4, 288, 128), f32)
        outs = pl.pallas_call(
            functools.partial(kernel, splits),
            out_shape=(
                big, big,
                jax.ShapeDtypeStruct((256, 64), f32),
                jax.ShapeDtypeStruct((9, 64, 64), f32),
                jax.ShapeDtypeStruct((64, 256), f32),
                jax.ShapeDtypeStruct((8, 128), f32),
            ),
            in_specs=[hbm] + [vmem] * 9 + [hbm],
            out_specs=(hbm, hbm, vmem, vmem, vmem, vmem),
            scratch_shapes=[
                pltpu.VMEM((2, 4, 288, 256), bf16),
                pltpu.VMEM((8, 288, 256), bf16),
                pltpu.VMEM((8, 288, 256), bf16),
                pltpu.VMEM((8, 288, 256), bf16),
                pltpu.VMEM((2, 256, 128), bf16),
                pltpu.VMEM((2, 128, 256), bf16),
                pltpu.VMEM((3, 384, 128), bf16),
                pltpu.VMEM((3, 128, 384), bf16),
                maps(), maps(), maps(), maps(),
                pltpu.VMEM((4, 288, 128), bf16),
                pltpu.VMEM((8, 288, 256), f32),
                pltpu.VMEM((8, 288, 256), f32),
                pltpu.VMEM((2, 4, 288, 256), bf16),
                maps(), maps(),
                pltpu.VMEM((4, 288, 128), bf16),
                pltpu.VMEM((2, 288, 128), bf16),
                pltpu.VMEM((2, 288, 128), bf16),
                pltpu.VMEM((2, 288, 128), bf16),
                pltpu.VMEM((2, 288, 128), bf16),
                pltpu.VMEM((6 * 288, 384), bf16),
                pltpu.VMEM((6 * 288, 384), bf16),
                pltpu.VMEM((6, 3, 8, 256), f32),
                pltpu.VMEM((ends, main_rows, 128), bf16),
                pltpu.VMEM((ends, main_rows, 128), bf16),
                pltpu.VMEM((ys, sub, 128), f32),
                pltpu.VMEM((ys, sub, 128), f32),
                pltpu.VMEM((zs, sub, 128), f32),
                pltpu.VMEM((ys, sub, 128), f32),
                pltpu.VMEM((ends, main_rows, 128), bf16),
                pltpu.VMEM((ends, late_rows, 128), bf16),
                pltpu.VMEM((ends, late_rows, 128), bf16),
                pltpu.VMEM((ys, late_rows, 128), bf16),
                pltpu.VMEM((zs, late_rows, 128), bf16),
                pltpu.VMEM((ends, late_rows, 128), bf16),
                pltpu.SemaphoreType.DMA((9,)),
                pltpu.SemaphoreType.DMA((2, 8)),
                pltpu.SemaphoreType.DMA((2, 2)),
                pltpu.SemaphoreType.DMA((2, 2)),
                pltpu.SemaphoreType.DMA((6, 2)),
                pltpu.SemaphoreType.DMA((6, 3)),
                pltpu.SemaphoreType.DMA((9, 12)),
                pltpu.SemaphoreType.DMA((9, 12)),
            ],
            compiler_params=pltpu.CompilerParams(
                collective_id=0, has_side_effects=True, vmem_limit_bytes=48 * 1024 * 1024
            ),
        )(
            images, wr, wd, we,
            g1.reshape(1, 64), s1.reshape(1, 64), g2.reshape(1, 64), s2.reshape(1, 64),
            g3.reshape(1, 256), s3.reshape(1, 256), cot,
        )
        res, gi, g_reduce, g_dilated, g_expand, vec = outs
        return (
            res, gi, g_reduce, g_dilated.reshape(3, 3, 64, 64), g_expand,
            vec[5, 0:64], vec[5, 64:128], vec[4, 0:64], vec[4, 64:128],
            vec[0:2].reshape(256), vec[2:4].reshape(256),
        )

    placed = (P("dp", "space", None, None),) + (P(),) * 9 + (P("dp", "space", None, None),)
    return jax.shard_map(
        shards,
        mesh=mesh,
        in_specs=placed,
        out_specs=(P("dp", "space", None, None),) * 2 + (P(),) * 9,
        check_vma=False,
    )
```

time: 738 us -> 96 us (0.13)
  waiting for transfers between devices: 473 us -> 0 us
  blocking collectives: 183 us -> 0 us
  Pallas kernels: 0 us -> 80.6 us
  other arithmetic: 21.2 us -> 0 us
  matrix products: 17.3 us -> 0 us
  between operations: 14.9 us -> 0.67 us
  starting transfers between devices: 10.6 us -> 0 us
    psum x1 -> x0, waiting for transfers between devices: 472 us -> none  [shards(): lax.psum((gw_reduce, gw_dilated, gw_expand, gg_one, gs_one, gg_two, gs_tw...]
    psum x10 -> x0, blocking collectives: 183 us -> none  [the longest x1 137 us: shards(): lax.psum((gw_reduce, gw_dilated, gw_expand, gg_one, gs_one, gg_two, gs_tw...]
    pallas_call x0 -> x1, Pallas kernels: none -> 80.6 us  [shards(): pl.pallas_call(functools.partial(kernel, splits), out_shape=(big, big, ja...]
    dot_general x33 -> x0, matrix products: 17.3 us -> none  [the longest x18 7.88 us: dilated(): jnp.dot(window, kernel[tap_row, tap_col], preferred_element_type=jnp.floa...]
    unnamed x68 -> x26, local copies, waits for them, and re-layouts: 0.95 us -> 13.1 us
    reshape x18 -> x1, local copies, waits for them, and re-layouts: 11.6 us -> 0.57 us  [shards(): vec[2:4].reshape(256)]
    ppermute x4 -> x0, starting transfers between devices: 10.6 us -> none  [the longest x2 7.98 us: extended(): lax.ppermute(lax.slice_in_dim(block, block.shape[dim] - width, None, axis...]
  transfers between devices with their start and end apart: 5 -> 0, of which waited for: 3 -> 0; matrix products, arithmetic and copies ran while one was open for 0% -> 0% of each run, Pallas kernels for 0% -> 0%
where the time goes in v1:
time: 96 us; the launch traced here: 95.6 us
  Pallas kernels  80.6 us (84%)
  local copies, waits for them, and re-layouts  14.3 us (15%)
    pallas_call x1, Pallas kernels, shards(): pl.pallas_call(functools.partial(kernel, splits), out_shape=(big, big, ja...  80.6 us
    unnamed x26, local copies, waits for them, and re-layouts  13.1 us

profile of v1, /device:TPU:1, one launch (start us, length us, event | category | flops | bytes accessed | tf_op | source)
XLA Modules:
  0.0 95.6 jit_solution(2843783991616988466)
XLA Ops:
  0.6 0.9 copy.22.wr
  1.5 0.0 copy-start
  1.5 1.3 %copy-done = bf16[1,8,288,256]{3,2,1,0:T(8,128)(2,1)S(1)} copy-done((bf16[1,8,288,256]{3,2,1,0:T(8,128)(2,1)S(1)}, bf16[1,8,288,256]{3,2,1,0:T(8,128)(2,1)}, u32[]{:S(2)}) %copy-start) | copy-done | bytes 1179672
  2.8 0.0 copy-start.1
  2.8 1.3 %copy-done.1 = bf16[1,8,288,256]{3,2,1,0:T(8,128)(2,1)S(1)} copy-done((bf16[1,8,288,256]{3,2,1,0:T(8,128)(2,1)S(1)}, bf16[1,8,288,256]{3,2,1,0:T(8,128)(2,1)}, u32[]{:S(2)}) %copy-start.1) | copy-done | bytes 1179672
  4.1 0.0 copy-start.2
  4.1 0.9 copy-done.2
  5.0 0.0 copy-start.3
  5.0 0.8 copy-done.3
  5.7 0.0 copy-start.4
  5.7 0.7 copy-done.4
  6.4 0.0 copy-start.5
  6.4 0.7 copy-done.5
  7.1 0.0 copy-start.6
  7.1 0.7 copy-done.6
  7.7 0.0 copy-start.7
  7.8 0.7 copy-done.7
  8.4 0.0 copy-start.8
  8.4 0.7 copy-done.8
  9.1 0.0 copy-start.9
  9.1 0.7 copy-done.9
  9.7 80.6 %shard_map.194 = (bf16[1,8,288,256]{3,2,1,0:T(8,128)(2,1)S(1)}, bf16[1,8,288,256]{3,2,1,0:T(8,128)(2,1)S(1)}, f32[256,64]{1,0:T(8,128)S(1)}, f32[9,64,64]{2,1,0:...) custom-call(bf16[1,8,288,256]{3,2,1,0:T(8,128)(2,1)S(1)} %copy-done, bf16[256,64]{1,0:T(8,128)(2,1)S(1)} %copy.22.wr, ...), custom_call_target="tpu_custom_call" | custom-call | tf_op jit(solution)/shard_map/pallas_call | solution.py:603
  90.4 0.6 slice_bitcast_fusion.2
  91.0 0.6 slice_bitcast_fusion
  91.5 0.7 copy.23
  92.2 1.0 %copy.28 = bf16[1,8,288,256]{3,2,1,0:T(8,128)(2,1)} copy(bf16[1,8,288,256]{3,2,1,0:T(8,128)(2,1)S(1)} %get-tuple-element.51) | data formatting | bytes 2359296
  93.3 1.0 %copy.29 = bf16[1,8,288,256]{3,2,1,0:T(8,128)(2,1)} copy(bf16[1,8,288,256]{3,2,1,0:T(8,128)(2,1)S(1)} %get-tuple-element.52) | data formatting | bytes 2359296
  94.3 0.7 copy.30
  95.0 0.6 copy.31
Async XLA Ops:
  1.5 1.3 %copy-start = (bf16[1,8,288,256]{3,2,1,0:T(8,128)(2,1)S(1)}, bf16[1,8,288,256]{3,2,1,0:T(8,128)(2,1)}, u32[]{:S(2)}) copy-start(bf16[1,8,288,256]{3,2,1,0:T(8,128)(2,1)} %images.1) | copy-start | bytes 3538948
  2.8 1.3 %copy-start.1 = (bf16[1,8,288,256]{3,2,1,0:T(8,128)(2,1)S(1)}, bf16[1,8,288,256]{3,2,1,0:T(8,128)(2,1)}, u32[]{:S(2)}) copy-start(bf16[1,8,288,256]{3,2,1,0:T(8,128)(2,1)} %cot.1) | copy-start | bytes 3538948
  4.1 0.9 copy-start.2
  5.0 0.8 copy-start.3
  5.7 0.7 copy-start.4
  6.4 0.7 copy-start.5
  7.1 0.7 copy-start.6
  7.7 0.7 copy-start.7
  8.4 0.7 copy-start.8
  9.1 0.7 copy-start.9

commit v2 on v1

--- a/solution.py
+++ b/solution.py
@@ -51,16 +51,16 @@
 
 def kernel(
     splits,
-    images, wr, wd, we, g1, s1, g2, s2, g3, s3, cot,
-    result, gimages, o_reduce, o_dilated, o_expand, o_vec,
-    img_v, cot_v, res_v, gi_v,
+    images, wr_h, wd_h, we_h, g1_h, s1_h, g2_h, s2_h, g3_h, s3_h, cot,
+    result, gimages, h_reduce, h_dilated, h_expand, h_vec,
+    res_v, gi_v, o_reduce, o_dilated, o_expand, o_vec, img_v, cot_v, wr, wd, we, g1, s1, g2, s2, g3, s3,
     w_in, w_out, w_fwd, w_bwd,
     pre1, slope1, pre2, slope2, act2, x3, e3, dh3, grad2, grad1, dh1,
     edge1, edge2, halo1, halo2, wide1, wide2,
-    xbuf,
+    xbuf, cross,
     main_a, main_ra, main_b, main_rb, main_c, main_gb, main_ga,
     late_a, late_ra, late_b, late_c, late_ga,
-    in_sem, out_sem, hs_sem, hr_sem, xs_sem, xr_sem, send_sem, recv_sem,
+    in_sem, out_sem, hs_sem, hr_sem, xs_sem, xr_sem, cs_sem, cr_sem, send_sem, recv_sem,
 ):
     ends, ys, highs = splits
     spaces = lax.axis_size("space")
@@ -92,23 +92,33 @@
         c = pltpu.make_async_copy(images.at[0, r], img_v.at[r % 2, r // 2], in_sem.at[r])
         c.start()
         in_copies.append(c)
+    small = []
+    pairs = (
+        (wr_h, wr), (wd_h, wd), (we_h, we), (g1_h, g1), (s1_h, s1),
+        (g2_h, g2), (s2_h, s2), (g3_h, g3), (s3_h, s3),
+    )
+    for k, (src, dst) in enumerate(pairs):
+        c = pltpu.make_async_copy(src, dst, in_sem.at[9 + k])
+        c.start()
+        small.append(c)
     cot_copy = pltpu.make_async_copy(cot.at[0], cot_v, in_sem.at[8])
     cot_copy.start()
 
     barrier = pltpu.get_barrier_semaphore()
     partners = 0
-    for name in "abc":
+    for name in "cba":
         n, me, ident = groups[name]
-        for k in range(1, n):
+        for k in sorted(range(1, n), key=lambda k: -min(k, n - k)):
             pl.semaphore_signal(
                 barrier, inc=1, device_id=ident(lax.rem(me + k, n)), device_id_type=MESH
             )
             partners += 1
 
-    zero_in = jnp.zeros((256, 64), bf16)
-    w_in[0] = jnp.concatenate([wr[...], zero_in], axis=1)
-    w_in[1] = jnp.concatenate([zero_in, wr[...]], axis=1)
+    for c in small:
+        c.wait()
     zero_out = jnp.zeros((64, 256), bf16)
+    w_in[0] = jnp.concatenate([wr[...], zero_out], axis=0)
+    w_in[1] = jnp.concatenate([zero_out, wr[...]], axis=0)
     w_out[0] = jnp.concatenate([we[...], zero_out], axis=0)
     w_out[1] = jnp.concatenate([zero_out, we[...]], axis=0)
     zero_mid = jnp.zeros((64, 64), bf16)
@@ -205,7 +215,7 @@
         wide[at : at + cols, 128:256] = x.astype(bf16)
         wide[at : at + cols, 256:384] = after.astype(bf16)
 
-    def take_halo(edge, halos, wide, which):
+    def take_halo(edge, halos, wide, which, finish):
         @pl.when(s > 0)
         def _():
             pltpu.make_async_remote_copy(
@@ -213,7 +223,7 @@
                 send_sem=hs_sem.at[which, 0], recv_sem=hr_sem.at[which, 0],
                 device_id=(d, s - 1), device_id_type=MESH,
             ).wait_recv()
-            widen(wide, 0, halos[0].astype(f32))
+            widen(wide, 0, finish(halos[0].astype(f32), s - 1))
 
         @pl.when(s < spaces - 1)
         def _():
@@ -222,7 +232,7 @@
                 send_sem=hs_sem.at[which, 1], recv_sem=hr_sem.at[which, 1],
                 device_id=(d, s + 1), device_id_type=MESH,
             ).wait_recv()
-            widen(wide, 5, halos[1].astype(f32))
+            widen(wide, 5, finish(halos[1].astype(f32), s + 1))
 
     def end_halo(edge, halos, which):
         @pl.when(s > 0)
@@ -253,8 +263,10 @@
             acc += dot_t(wide2[(pair + a) * cols : (pair + a + n) * cols, :], w_bwd[a])
         return acc
 
-    def local_moments(idx, pre, acc):
+    def local_moments(idx, pre, acc, early=None):
         mean = both(acc) * (1.0 / local)
+        if early is not None:
+            early(mean)
         sq = jnp.zeros((8, 128), f32)
         for p in range(4):
             c = pre[p] - mean
@@ -294,36 +306,69 @@
     for p in range(4):
         in_copies[2 * p].wait()
         in_copies[2 * p + 1].wait()
-        v = dotf(img_v[0, p], w_in[0]) + dotf(img_v[1, p], w_in[1])
+        v = dot_t(img_v[0, p], w_in[0]) + dot_t(img_v[1, p], w_in[1])
         pre1[p] = v
         acc += part_sum(v)
     gain1, shift1 = twice(g1), twice(s1)
     gain2, shift2 = twice(g2), twice(s2)
     pl.semaphore_wait(barrier, partners)
-    local_moments(0, pre1, acc)
-    mu, istd1 = moments(0, 128)
-    for p in (0, 3, 1, 2):
+
+    def early(mean):
+        edge1[0] = (pre1[0] - mean).astype(bf16)
+        edge1[1] = (pre1[3] - mean).astype(bf16)
+        halo(edge1, halo1, 0)
+
+    local_moments(0, pre1, acc, early)
+    image_sum = jnp.zeros((8, 256), f32)
+    for q in range(2):
+        for p in range(4):
+            image_sum += part_sum(img_v[q, p].astype(f32))
+    image_sum = total(image_sum)
+    mu1, istd1 = moments(0, 128)
+    mu = mu1
+    for p in range(4):
         xhat = (pre1[p] - mu) * istd1
         act, slope = gates(gain1 * xhat + shift1)
         pre1[p] = xhat
         slope1[p] = slope
-        if p == 0:
-            edge1[0] = act.astype(bf16)
-        if p == 3:
-            edge1[1] = act.astype(bf16)
-            halo(edge1, halo1, 0)
         widen(wide1, p + 1, act)
 
     v = conv_fwd(1, 2)
     pre2[1] = v[0:cols]
     pre2[2] = v[cols : 2 * cols]
     acc = part_sum(v)
-    take_halo(edge1, halo1, wide1, 0)
+
+    def halo_act(c, f):
+        xhat = (c + (xbuf[0, f, 0:1, 0:128] - mu1)) * istd1
+        return gates(gain1 * xhat + shift1)[0]
+
+    take_halo(edge1, halo1, wide1, 0, halo_act)
     for p in (0, 3):
         v = conv_fwd(p, 1)
         pre2[p] = v
         acc += part_sum(v)
     local_moments(1, pre2, acc)
+
+    rows = 4 * cols
+    xhat = pre1[...].reshape(rows, 128).T
+    xhat_high = xhat.astype(bf16)
+    xhat_low = (xhat - xhat_high.astype(f32)).astype(bf16)
+    even, odd = img_v[0].reshape(rows, 256), img_v[1].reshape(rows, 256)
+    cross[s, 0:64, :] = (
+        dotf(xhat_high[0:64], even) + dotf(xhat_high[64:128], odd)
+        + dotf(xhat_low[0:64], even) + dotf(xhat_low[64:128], odd)
+    )
+    cross[s, 64:72, :] = jnp.broadcast_to(image_sum, (8, 256))
+
+    def cross_copy(k):
+        return pltpu.make_async_remote_copy(
+            src_ref=cross.at[s], dst_ref=cross.at[s],
+            send_sem=cs_sem.at[k], recv_sem=cr_sem.at[s],
+            device_id=(d, lax.rem(s + k, spaces)), device_id_type=MESH,
+        )
+
+    for k in range(1, 3):
+        cross_copy(k).start()
     mu, istd2 = moments(1, 128)
     acc3 = jnp.zeros((8, 256), f32)
     for p in range(4):
@@ -356,10 +401,10 @@
         xhat = (x3[r] - mu) * istd3
         act, slope = gates(gain3 * xhat + shift3 + img_v[q, p].astype(f32))
         res_v[r] = act.astype(bf16)
+        pltpu.make_async_copy(res_v.at[r], result.at[0, r], out_sem.at[0, r]).start()
         e = cot_v[r].astype(f32) * slope
         x3[r] = xhat
         e3[r] = e
-        pltpu.make_async_copy(res_v.at[r], result.at[0, r], out_sem.at[0, r]).start()
         return sd + part_sum(e), sx + part_sum(e * xhat)
 
     zero8 = jnp.zeros((8, 256), f32)
@@ -383,7 +428,6 @@
         sx_acc += part_sum(g * pre2[p])
     sd2, sx2 = both(sd_acc), both(sx_acc)
     send_stats(4, sd2, sx2)
-    rows = 4 * cols
     act_t = act2[...].reshape(rows, 128).T
     expand = dotf(act_t[0:64], dh3[0].reshape(rows, 256)) + dotf(
         act_t[64:128], dh3[1].reshape(rows, 256)
@@ -413,7 +457,7 @@
     v = conv_bwd(1, 2)
     sd_acc, sx_acc = first_back(1, v[0:cols], sd_acc, sx_acc)
     sd_acc, sx_acc = first_back(2, v[cols : 2 * cols], sd_acc, sx_acc)
-    take_halo(edge2, halo2, wide2, 1)
+    take_halo(edge2, halo2, wide2, 1, lambda c, f: c)
     for p in (0, 3):
         sd_acc, sx_acc = first_back(p, conv_bwd(p, 1), sd_acc, sx_acc)
     sd1, sx1 = both(sd_acc), both(sx_acc)
@@ -466,16 +510,29 @@
     a_src, a_dst = (lambda t: main_a.at[t]), (lambda me: main_ra.at[me])
     spread_out(0, "a", a_src, a_dst)
 
-    sd, sx = sums(5, 128)
     k0 = gain1 * istd1
-    k1 = k0 * sd * (1.0 / count)
-    k2 = k0 * sx * (1.0 / count)
+    own_sd = sd1 * (1.0 / local)
+    own_sx = sx1 * (1.0 / local)
     for p in range(4):
-        dh1[p] = (k0 * grad1[p] - k1 - k2 * pre1[p]).astype(bf16)
-    dh1_t = dh1[...].reshape(rows, 128).T
-    reduce = dotf(dh1_t[0:64], img_v[0].reshape(rows, 256)) + dotf(
-        dh1_t[64:128], img_v[1].reshape(rows, 256)
+        dh1[p] = (k0 * (grad1[p] - own_sd - pre1[p] * own_sx)).astype(bf16)
+    rest_t = dh1[...].reshape(rows, 128).T
+    reduce = dotf(rest_t[0:64], img_v[0].reshape(rows, 256)) + dotf(
+        rest_t[64:128], img_v[1].reshape(rows, 256)
     )
+    for k in range(1, 3):
+        f = lax.rem(s + k, spaces)
+        pltpu.make_async_remote_copy(
+            src_ref=cross.at[f], dst_ref=cross.at[f],
+            send_sem=cs_sem.at[k], recv_sem=cr_sem.at[f],
+            device_id=(d, f), device_id_type=MESH,
+        ).wait_recv()
+    excess = cross[s] * (1.0 / local) - (cross[0] + cross[1] + cross[2]) * (1.0 / count)
+
+    def down(row):
+        column = jnp.broadcast_to(row, (128, 128)).T[0:64]
+        return jnp.concatenate([column, column], axis=1)
+
+    reduce += down(k0 * sd1) * excess[64:65] + down(k0 * sx1) * excess[0:64]
     for h in range(2):
         for piece in range(ends):
             lo, hi = piece * late_rows, (piece + 1) * late_rows
@@ -488,14 +545,6 @@
     la_src, la_dst = (lambda t: late_a.at[t]), (lambda me: late_ra.at[me])
     spread_out(5, "a", la_src, la_dst)
 
-    def last(p, carry):
-        dh = dh1[p]
-        for q in range(2):
-            r = 2 * p + q
-            gi_v[r] = (dot_t(dh, w_in[q]) + e3[r]).astype(bf16)
-            pltpu.make_async_copy(gi_v.at[r], gimages.at[0, r], out_sem.at[1, r]).start()
-        return carry
-
     collect(0, "a", a_src, a_dst)
     part = added(main_ra, ends)
     sub = main_rows // ys
@@ -505,6 +554,18 @@
     b_src, b_dst = (lambda t: main_b.at[t]), (lambda me: main_rb.at[me])
     spread_out(1, "b", b_src, b_dst)
 
+    sd, sx = sums(5, 128)
+    k1 = k0 * sd * (1.0 / count)
+    k2 = k0 * sx * (1.0 / count)
+
+    def last(p, carry):
+        dh = (k0 * grad1[p] - k1 - k2 * pre1[p]).astype(bf16)
+        for q in range(2):
+            r = 2 * p + q
+            gi_v[r] = (dotf(dh, w_in[q]) + e3[r]).astype(bf16)
+            pltpu.make_async_copy(gi_v.at[r], gimages.at[0, r], out_sem.at[1, r]).start()
+        return carry
+
     lax.fori_loop(0, 2, last, 0)
 
     collect(5, "a", la_src, la_dst)
@@ -550,9 +611,9 @@
 
     scale = 1.0 / lax.axis_size("dp")
     collect(8, "a", lg_src, lg_dst)
-    late = late_ga[...].reshape(LATE_ROWS, 128).astype(f32).T * scale
-    o_reduce[0:128, :] = late[:, 0:64]
-    o_reduce[128:256, :] = late[:, 64:128]
+    late = late_ga[...].reshape(LATE_ROWS, 128).astype(f32) * scale
+    o_reduce[:, 0:128] = late[0:64]
+    o_reduce[:, 128:256] = late[64:128]
 
     collect(4, "a", ga_src, ga_dst)
     main = main_ga[...].reshape(MAIN_ROWS, 128).astype(f32) * scale
@@ -566,6 +627,13 @@
     o_expand[:, 128:256] = main[384:448]
     o_vec[...] = main[VEC : VEC + 8] + main[VEC + 8 : VEC + 16]
 
+    outs = []
+    for k, (src, dst) in enumerate(
+        ((o_reduce, h_reduce), (o_dilated, h_dilated), (o_expand, h_expand), (o_vec, h_vec))
+    ):
+        outs.append(pltpu.make_async_copy(src, dst, out_sem.at[2, k]))
+        outs[-1].start()
+
     for idx in range(6):
         for k in range(1, 3):
             pltpu.make_async_remote_copy(
@@ -573,6 +641,8 @@
                 send_sem=xs_sem.at[idx, k - 1], recv_sem=xr_sem.at[idx, s],
                 device_id=(d, lax.rem(s + k, spaces)), device_id_type=MESH,
             ).wait_send()
+    for k in range(1, 3):
+        cross_copy(k).wait_send()
     end_halo(edge1, halo1, 0)
     end_halo(edge2, halo2, 1)
     for stage, name, src, dst in (
@@ -585,6 +655,39 @@
     for r in range(8):
         pltpu.make_async_copy(res_v.at[r], result.at[0, r], out_sem.at[0, r]).wait()
         pltpu.make_async_copy(gi_v.at[r], gimages.at[0, r], out_sem.at[1, r]).wait()
+    for c in outs:
+        c.wait()
+
+
+def store(*refs):
+    ins, outs, (half, full, vec, sem) = refs[:6], refs[6:17], refs[17:]
+    fetch = pltpu.make_async_copy(ins[5], vec, sem.at[19])
+    fetch.start()
+    copies = []
+    for k in range(2):
+        for r in range(4):
+            rows = pl.ds(2 * r, 2)
+            copies.append(
+                pltpu.make_async_copy(ins[k].at[0, rows], outs[k].at[0, rows], sem.at[11 + 4 * k + r])
+            )
+    copies += [pltpu.make_async_copy(ins[k], outs[k], sem.at[k]) for k in range(2, 5)]
+    for c in copies:
+        c.start()
+    fetch.wait()
+    for k, row in enumerate((5, 4)):
+        v = vec[row : row + 1, :]
+        half[2 * k] = v[:, 0:64]
+        half[2 * k + 1] = pltpu.roll(jnp.broadcast_to(v, (8, 128)), 64, 1)[0:1, 0:64]
+    for k in range(2):
+        full[k] = jnp.concatenate([vec[2 * k : 2 * k + 1, :], vec[2 * k + 1 : 2 * k + 2, :]], axis=1)
+    for k in range(4):
+        copies.append(pltpu.make_async_copy(half.at[k], outs[5 + k], sem.at[5 + k]))
+        copies[-1].start()
+    for k in range(2):
+        copies.append(pltpu.make_async_copy(full.at[k], outs[9 + k], sem.at[9 + k]))
+        copies[-1].start()
+    for c in copies:
+        c.wait()
 
 
 def solution(mesh):
@@ -597,26 +700,36 @@
 
     def shards(images, wr, wd, we, g1, s1, g2, s2, g3, s3, cot):
         vmem = pl.BlockSpec(memory_space=pltpu.VMEM)
-        hbm = pl.BlockSpec(memory_space=pl.ANY)
+        hbm = pl.BlockSpec(memory_space=pltpu.HBM)
         big = jax.ShapeDtypeStruct(images.shape, bf16)
         maps = lambda: pltpu.VMEM((4, 288, 128), f32)
         outs = pl.pallas_call(
             functools.partial(kernel, splits),
             out_shape=(
                 big, big,
-                jax.ShapeDtypeStruct((256, 64), f32),
+                jax.ShapeDtypeStruct((64, 256), f32),
                 jax.ShapeDtypeStruct((9, 64, 64), f32),
                 jax.ShapeDtypeStruct((64, 256), f32),
                 jax.ShapeDtypeStruct((8, 128), f32),
             ),
-            in_specs=[hbm] + [vmem] * 9 + [hbm],
-            out_specs=(hbm, hbm, vmem, vmem, vmem, vmem),
+            in_specs=[hbm] * 11,
+            out_specs=(hbm,) * 6,
             scratch_shapes=[
+                pltpu.VMEM((8, 288, 256), bf16),
+                pltpu.VMEM((8, 288, 256), bf16),
+                pltpu.VMEM((64, 256), f32),
+                pltpu.VMEM((9, 64, 64), f32),
+                pltpu.VMEM((64, 256), f32),
+                pltpu.VMEM((8, 128), f32),
                 pltpu.VMEM((2, 4, 288, 256), bf16),
                 pltpu.VMEM((8, 288, 256), bf16),
-                pltpu.VMEM((8, 288, 256), bf16),
-                pltpu.VMEM((8, 288, 256), bf16),
-                pltpu.VMEM((2, 256, 128), bf16),
+                pltpu.VMEM((64, 256), bf16),
+                pltpu.VMEM((3, 3, 64, 64), bf16),
+                pltpu.VMEM((64, 256), bf16),
+                pltpu.VMEM((1, 64), f32), pltpu.VMEM((1, 64), f32),
+                pltpu.VMEM((1, 64), f32), pltpu.VMEM((1, 64), f32),
+                pltpu.VMEM((1, 256), f32), pltpu.VMEM((1, 256), f32),
+                pltpu.VMEM((2, 128, 256), bf16),
                 pltpu.VMEM((2, 128, 256), bf16),
                 pltpu.VMEM((3, 384, 128), bf16),
                 pltpu.VMEM((3, 128, 384), bf16),
@@ -634,6 +747,7 @@
                 pltpu.VMEM((6 * 288, 384), bf16),
                 pltpu.VMEM((6 * 288, 384), bf16),
                 pltpu.VMEM((6, 3, 8, 256), f32),
+                pltpu.VMEM((3, 72, 256), f32),
                 pltpu.VMEM((ends, main_rows, 128), bf16),
                 pltpu.VMEM((ends, main_rows, 128), bf16),
                 pltpu.VMEM((ys, sub, 128), f32),
@@ -646,28 +760,44 @@
                 pltpu.VMEM((ys, late_rows, 128), bf16),
                 pltpu.VMEM((zs, late_rows, 128), bf16),
                 pltpu.VMEM((ends, late_rows, 128), bf16),
-                pltpu.SemaphoreType.DMA((9,)),
-                pltpu.SemaphoreType.DMA((2, 8)),
+                pltpu.SemaphoreType.DMA((18,)),
+                pltpu.SemaphoreType.DMA((3, 8)),
                 pltpu.SemaphoreType.DMA((2, 2)),
                 pltpu.SemaphoreType.DMA((2, 2)),
                 pltpu.SemaphoreType.DMA((6, 2)),
                 pltpu.SemaphoreType.DMA((6, 3)),
+                pltpu.SemaphoreType.DMA((3,)),
+                pltpu.SemaphoreType.DMA((3,)),
                 pltpu.SemaphoreType.DMA((9, 12)),
                 pltpu.SemaphoreType.DMA((9, 12)),
             ],
             compiler_params=pltpu.CompilerParams(
-                collective_id=0, has_side_effects=True, vmem_limit_bytes=48 * 1024 * 1024
+                collective_id=0, has_side_effects=True, vmem_limit_bytes=60 * 1024 * 1024
             ),
         )(
-            images, wr, wd, we,
+            images, wr.T, wd, we,
             g1.reshape(1, 64), s1.reshape(1, 64), g2.reshape(1, 64), s2.reshape(1, 64),
             g3.reshape(1, 256), s3.reshape(1, 256), cot,
         )
-        res, gi, g_reduce, g_dilated, g_expand, vec = outs
+        res, gi, g_reduce, g_dilated, g_expand, v1, v2, v3, v4, v5, v6 = pl.pallas_call(
+            store,
+            out_shape=tuple(jax.ShapeDtypeStruct(x.shape, x.dtype) for x in outs[:5])
+            + (jax.ShapeDtypeStruct((1, 64), f32),) * 4
+            + (jax.ShapeDtypeStruct((1, 256), f32),) * 2,
+            in_specs=[hbm] * 6,
+            out_specs=(hbm,) * 11,
+            scratch_shapes=[
+                pltpu.VMEM((4, 1, 64), f32),
+                pltpu.VMEM((2, 1, 256), f32),
+                pltpu.VMEM((8, 128), f32),
+                pltpu.SemaphoreType.DMA((20,)),
+            ],
+            compiler_params=pltpu.CompilerParams(vmem_limit_bytes=60 * 1024 * 1024),
+        )(*outs)
         return (
-            res, gi, g_reduce, g_dilated.reshape(3, 3, 64, 64), g_expand,
-            vec[5, 0:64], vec[5, 64:128], vec[4, 0:64], vec[4, 64:128],
-            vec[0:2].reshape(256), vec[2:4].reshape(256),
+            res, gi, g_reduce.T, g_dilated.reshape(3, 3, 64, 64), g_expand,
+            v1.reshape(64), v2.reshape(64), v3.reshape(64), v4.reshape(64),
+            v5.reshape(256), v6.reshape(256),
         )
 
     placed = (P("dp", "space", None, None),) + (P(),) * 9 + (P("dp", "space", None, None),)

time: 96 us -> 162 us (1.69)
  Pallas kernels: 80.6 us -> 161 us
  local copies, waits for them, and re-layouts: 14.3 us -> 0 us
    pallas_call x0 -> x1, Pallas kernels: none -> 85.7 us  [shards(): pl.pallas_call(store, out_shape=tuple((jax.ShapeDtypeStruct(x.shape, x.dt...]
    unnamed x26 -> x0, local copies, waits for them, and re-layouts: 13.1 us -> none
    pallas_call x1, Pallas kernels: 80.6 us -> 75.5 us  [shards(): pl.pallas_call(functools.partial(kernel, splits), out_shape=(big, big, ja...]
where the time goes in v2:
time: 162 us
  Pallas kernels  161 us (99%)
    pallas_call x1, Pallas kernels, shards(): pl.pallas_call(store, out_shape=tuple((jax.ShapeDtypeStruct(x.shape, x.dt...  85.7 us
    pallas_call x1, Pallas kernels, shards(): pl.pallas_call(functools.partial(kernel, splits), out_shape=(big, big, ja...  75.5 us

profile of v2, /device:TPU:1, one launch (start us, length us, event | category | flops | bytes accessed | tf_op | source)
XLA Modules:
  0.0 161.8 jit_solution(15886861306009321557)
XLA Ops:
  0.6 75.5 %shard_map.194 = (bf16[1,8,288,256]{3,2,1,0:T(8,128)(2,1)}, bf16[1,8,288,256]{3,2,1,0:T(8,128)(2,1)}, f32[64,256]{1,0:T(8,128)}, f32[9,64,64]{2,1,0:T(8,128)}, f32[64,256]{1,0:T(8,128)}, /*index=5*/f32[8,128]{1,0:T(8,128)}) custom-call(bf16[1,8,288,256]{3,2,1,0:T(8,128)(2,1)} %images.1, bf16[64,256]{1,0:T(8,128)(2,1)} %bitcast.15, ...), custom_call_target="tpu_custom_call" | custom-call | tf_op jit(solution)/shard_map/pallas_call | solution.py:706
  76.1 85.7 %shard_map.195 = (bf16[1,8,288,256]{3,2,1,0:T(8,128)(2,1)}, bf16[1,8,288,256]{3,2,1,0:T(8,128)(2,1)}, f32[64,256]{1,0:T(8,128)}, f32[9,64,64]{2,1,0:T(8,128)}, f...) custom-call(bf16[1,8,288,256]{3,2,1,0:T(8,128)(2,1)} %get-tuple-elem, ...), custom_call_target="tpu_custom_call" | custom-call | tf_op jit(solution)/shard_map/pallas_call | solution.py:782

commit v3 on v2

--- a/solution.py
+++ b/solution.py
@@ -660,20 +660,24 @@
 
 
 def store(*refs):
-    ins, outs, (half, full, vec, sem) = refs[:6], refs[6:17], refs[17:]
-    fetch = pltpu.make_async_copy(ins[5], vec, sem.at[19])
-    fetch.start()
-    copies = []
+    ins, outs, held, (half, full, sem) = refs[:6], refs[6:17], refs[17:23], refs[23:]
+    vec = held[5]
+    parts = []
     for k in range(2):
         for r in range(4):
             rows = pl.ds(2 * r, 2)
-            copies.append(
-                pltpu.make_async_copy(ins[k].at[0, rows], outs[k].at[0, rows], sem.at[11 + 4 * k + r])
-            )
-    copies += [pltpu.make_async_copy(ins[k], outs[k], sem.at[k]) for k in range(2, 5)]
-    for c in copies:
+            parts.append((ins[k].at[0, rows], held[k].at[0, rows], outs[k].at[0, rows]))
+    parts += [(ins[k], held[k], outs[k]) for k in range(2, 5)]
+    fetches = [pltpu.make_async_copy(p[0], p[1], sem.at[0, k]) for k, p in enumerate(parts)]
+    fetches.append(pltpu.make_async_copy(ins[5], vec, sem.at[0, 11]))
+    for c in fetches:
         c.start()
-    fetch.wait()
+    copies = []
+    for k, p in enumerate(parts):
+        fetches[k].wait()
+        copies.append(pltpu.make_async_copy(p[1], p[2], sem.at[1, k]))
+        copies[-1].start()
+    fetches[-1].wait()
     for k, row in enumerate((5, 4)):
         v = vec[row : row + 1, :]
         half[2 * k] = v[:, 0:64]
@@ -681,10 +685,10 @@
     for k in range(2):
         full[k] = jnp.concatenate([vec[2 * k : 2 * k + 1, :], vec[2 * k + 1 : 2 * k + 2, :]], axis=1)
     for k in range(4):
-        copies.append(pltpu.make_async_copy(half.at[k], outs[5 + k], sem.at[5 + k]))
+        copies.append(pltpu.make_async_copy(half.at[k], outs[5 + k], sem.at[1, 11 + k]))
         copies[-1].start()
     for k in range(2):
-        copies.append(pltpu.make_async_copy(full.at[k], outs[9 + k], sem.at[9 + k]))
+        copies.append(pltpu.make_async_copy(full.at[k], outs[9 + k], sem.at[1, 15 + k]))
         copies[-1].start()
     for c in copies:
         c.wait()
@@ -786,11 +790,10 @@
             + (jax.ShapeDtypeStruct((1, 256), f32),) * 2,
             in_specs=[hbm] * 6,
             out_specs=(hbm,) * 11,
-            scratch_shapes=[
+            scratch_shapes=[pltpu.VMEM(x.shape, x.dtype) for x in outs] + [
                 pltpu.VMEM((4, 1, 64), f32),
                 pltpu.VMEM((2, 1, 256), f32),
-                pltpu.VMEM((8, 128), f32),
-                pltpu.SemaphoreType.DMA((20,)),
+                pltpu.SemaphoreType.DMA((2, 17)),
             ],
             compiler_params=pltpu.CompilerParams(vmem_limit_bytes=60 * 1024 * 1024),
         )(*outs)

time: 162 us -> 79.1 us (0.49)
  Pallas kernels: 161 us -> 78.3 us
    pallas_call x1, Pallas kernels: 85.7 us -> 2.8 us  [shards(): pl.pallas_call(store, out_shape=tuple((jax.ShapeDtypeStruct(x.shape, x.dt...]
where the time goes in v3:
time: 79.1 us; the launch traced here: 78.9 us
  Pallas kernels  78.3 us (99%)
    pallas_call x1, Pallas kernels, shards(): pl.pallas_call(functools.partial(kernel, splits), out_shape=(big, big, ja...  75.5 us
    pallas_call x1, Pallas kernels, shards(): pl.pallas_call(store, out_shape=tuple((jax.ShapeDtypeStruct(x.shape, x.dt...  2.8 us

profile of v3, /device:TPU:1, one launch (start us, length us, event | category | flops | bytes accessed | tf_op | source)
XLA Modules:
  0.0 78.9 jit_solution(15136833170576409563)
XLA Ops:
  0.6 75.5 %shard_map.194 = (bf16[1,8,288,256]{3,2,1,0:T(8,128)(2,1)}, bf16[1,8,288,256]{3,2,1,0:T(8,128)(2,1)}, f32[64,256]{1,0:T(8,128)}, f32[9,64,64]{2,1,0:T(8,128)}, f32[64,256]{1,0:T(8,128)}, /*index=5*/f32[8,128]{1,0:T(8,128)}) custom-call(bf16[1,8,288,256]{3,2,1,0:T(8,128)(2,1)} %images.1, bf16[64,256]{1,0:T(8,128)(2,1)} %bitcast.15, ...), custom_call_target="tpu_custom_call" | custom-call | tf_op jit(solution)/shard_map/pallas_call | solution.py:710
  76.1 2.8 %shard_map.195 = (bf16[1,8,288,256]{3,2,1,0:T(8,128)(2,1)}, bf16[1,8,288,256]{3,2,1,0:T(8,128)(2,1)}, f32[64,256]{1,0:T(8,128)}, f32[9,64,64]{2,1,0:T(8,128)}, f...) custom-call(bf16[1,8,288,256]{3,2,1,0:T(8,128)(2,1)} %get-tuple-elem, ...), custom_call_target="tpu_custom_call" | custom-call | tf_op jit(solution)/shard_map/pallas_call | solution.py:786

commit v4 on v3

--- a/solution.py
+++ b/solution.py
@@ -15,7 +15,6 @@
 SPLITS = {256: (8, 8, 4), 4: (2, 2, 1)}
 MAIN_ROWS = 512
 LATE_ROWS = 128
-VEC = 448
 
 
 def part_sum(x):
@@ -56,10 +55,11 @@
     res_v, gi_v, o_reduce, o_dilated, o_expand, o_vec, img_v, cot_v, wr, wd, we, g1, s1, g2, s2, g3, s3,
     w_in, w_out, w_fwd, w_bwd,
     pre1, slope1, pre2, slope2, act2, x3, e3, dh3, grad2, grad1, dh1,
-    edge1, edge2, halo1, halo2, wide1, wide2,
-    xbuf, cross,
+    edge1, edge2, edge3, halo1, halo2, halo3, wide1, wide2,
+    xbuf, cross, cross2, excess1, excess2,
     main_a, main_ra, main_b, main_rb, main_c, main_gb, main_ga,
     late_a, late_ra, late_b, late_c, late_ga,
+    vec_a, vec_b, vec_c,
     in_sem, out_sem, hs_sem, hr_sem, xs_sem, xr_sem, cs_sem, cr_sem, send_sem, recv_sem,
 ):
     ends, ys, highs = splits
@@ -68,10 +68,11 @@
     d = lax.axis_index("dp")
     s = lax.axis_index("space")
     end = lax.rem(d, ends)
-    high = lax.rem(lax.div(d, ends), highs)
+    upper = lax.rem(lax.div(d, ends), highs)
     y = lax.div(d, ends * highs)
-    z = high * spaces + s
+    z = upper * spaces + s
     cols = 288
+    before, after = s - 1, s + 1
     local = 2304.0
     count = local * spaces
 
@@ -83,7 +84,7 @@
 
     def id_c(k):
         kh = lax.div(k, spaces)
-        return (d + (kh - high) * ends, lax.rem(k, spaces))
+        return (d + (kh - upper) * ends, lax.rem(k, spaces))
 
     groups = {"a": (ends, end, id_a), "b": (ys, y, id_b), "c": (zs, z, id_c)}
 
@@ -209,11 +210,11 @@
     def widen(wide, pair, x):
         at = pair * cols
         spot = lax.broadcasted_iota(jnp.int32, (cols, 128), 0)
-        before = jnp.where(spot >= 2, pltpu.roll(x, 2, 0), 0.0)
-        after = jnp.where(spot < cols - 2, pltpu.roll(x, cols - 2, 0), 0.0)
-        wide[at : at + cols, 0:128] = before.astype(bf16)
+        left = jnp.where(spot >= 2, pltpu.roll(x, 2, 0), 0.0)
+        right = jnp.where(spot < cols - 2, pltpu.roll(x, cols - 2, 0), 0.0)
+        wide[at : at + cols, 0:128] = left.astype(bf16)
         wide[at : at + cols, 128:256] = x.astype(bf16)
-        wide[at : at + cols, 256:384] = after.astype(bf16)
+        wide[at : at + cols, 256:384] = right.astype(bf16)
 
     def take_halo(edge, halos, wide, which, finish):
         @pl.when(s > 0)
@@ -223,7 +224,8 @@
                 send_sem=hs_sem.at[which, 0], recv_sem=hr_sem.at[which, 0],
                 device_id=(d, s - 1), device_id_type=MESH,
             ).wait_recv()
-            widen(wide, 0, finish(halos[0].astype(f32), s - 1))
+            if wide is not None:
+                widen(wide, 0, finish(halos[0].astype(f32), before))
 
         @pl.when(s < spaces - 1)
         def _():
@@ -232,7 +234,8 @@
                 send_sem=hs_sem.at[which, 1], recv_sem=hr_sem.at[which, 1],
                 device_id=(d, s + 1), device_id_type=MESH,
             ).wait_recv()
-            widen(wide, 5, finish(halos[1].astype(f32), s + 1))
+            if wide is not None:
+                widen(wide, 5, finish(halos[1].astype(f32), after))
 
     def end_halo(edge, halos, which):
         @pl.when(s > 0)
@@ -272,6 +275,52 @@
             c = pre[p] - mean
             sq += part_sum(c * c)
         send_stats(idx, mean, both(sq))
+        return mean
+
+    def high_low(x):
+        high = x.astype(bf16)
+        low = (x - high.astype(f32)).astype(bf16)
+        return high.T, low.T
+
+    def folded(g):
+        taps = []
+        for t in range(9):
+            a, b = divmod(t, 3)
+            block = g[a][:, b * 128 : (b + 1) * 128]
+            n = block.shape[0] // 2 if block.shape[0] > 8 else 8
+            even, odd = block[0:n], block[block.shape[0] - n :]
+            if t % 2 == 0:
+                taps.append(even + pltpu.roll(odd, 64, 1))
+            else:
+                taps.append(pltpu.roll(even, 64, 1) + odd)
+        taps.append(jnp.zeros_like(taps[0]))
+        low = lax.broadcasted_iota(jnp.int32, taps[0].shape, 1) < 64
+        return [jnp.where(low, taps[2 * u], taps[2 * u + 1]) for u in range(5)]
+
+    def down(row):
+        return jnp.broadcast_to(row, (128, 128)).T[0:64]
+
+    def down2(row):
+        return jnp.concatenate([down(row)] * 2, axis=1)
+
+    def cross_copy(which, buf, k):
+        return pltpu.make_async_remote_copy(
+            src_ref=buf.at[s], dst_ref=buf.at[s],
+            send_sem=cs_sem.at[which, k], recv_sem=cr_sem.at[which, s],
+            device_id=(d, lax.rem(s + k, spaces)), device_id_type=MESH,
+        )
+
+    def take_cross(which, buf):
+        for k in range(1, 3):
+            f = lax.rem(s + k, spaces)
+            pltpu.make_async_remote_copy(
+                src_ref=buf.at[f], dst_ref=buf.at[f],
+                send_sem=cs_sem.at[which, k], recv_sem=cr_sem.at[which, f],
+                device_id=(d, f), device_id_type=MESH,
+            ).wait_recv()
+
+    rows = 4 * cols
+    ones = jnp.ones((16, rows), bf16)
 
     def copy_to(stage, name, src, dst, k):
         n, me, ident = groups[name]
@@ -318,12 +367,17 @@
         edge1[1] = (pre1[3] - mean).astype(bf16)
         halo(edge1, halo1, 0)
 
-    local_moments(0, pre1, acc, early)
-    image_sum = jnp.zeros((8, 256), f32)
+    mean1 = local_moments(0, pre1, acc, early)
+
+    high, low = high_low(pre1[...].reshape(rows, 128) - mean1)
+    crossed = jnp.zeros((144, 256), f32)
     for q in range(2):
-        for p in range(4):
-            image_sum += part_sum(img_v[q, p].astype(f32))
-    image_sum = total(image_sum)
+        left = jnp.concatenate([high[64 * q : 64 * q + 64], low[64 * q : 64 * q + 64], ones], axis=0)
+        crossed += dotf(left, img_v[q].reshape(rows, 256))
+    cross[s, 0:64, :] = crossed[0:64] + crossed[64:128]
+    cross[s, 64:72, :] = crossed[128:136]
+    for k in range(1, 3):
+        cross_copy(0, cross, k).start()
     mu1, istd1 = moments(0, 128)
     mu = mu1
     for p in range(4):
@@ -347,35 +401,30 @@
         v = conv_fwd(p, 1)
         pre2[p] = v
         acc += part_sum(v)
-    local_moments(1, pre2, acc)
-
-    rows = 4 * cols
-    xhat = pre1[...].reshape(rows, 128).T
-    xhat_high = xhat.astype(bf16)
-    xhat_low = (xhat - xhat_high.astype(f32)).astype(bf16)
-    even, odd = img_v[0].reshape(rows, 256), img_v[1].reshape(rows, 256)
-    cross[s, 0:64, :] = (
-        dotf(xhat_high[0:64], even) + dotf(xhat_high[64:128], odd)
-        + dotf(xhat_low[0:64], even) + dotf(xhat_low[64:128], odd)
-    )
-    cross[s, 64:72, :] = jnp.broadcast_to(image_sum, (8, 256))
-
-    def cross_copy(k):
-        return pltpu.make_async_remote_copy(
-            src_ref=cross.at[s], dst_ref=cross.at[s],
-            send_sem=cs_sem.at[k], recv_sem=cr_sem.at[s],
-            device_id=(d, lax.rem(s + k, spaces)), device_id_type=MESH,
-        )
-
+    mean2 = local_moments(1, pre2, acc)
+
+    high, low = high_low(pre2[...].reshape(rows, 128) - mean2)
+    left = jnp.concatenate([high, low, ones], axis=0)
+    crossed = [dotf(left, wide1[a * cols : a * cols + rows, :]) for a in range(3)]
+    sides = folded([c[0:128] + c[128:256] for c in crossed])
+    plain = folded([c[256:264] for c in crossed])
+    for u in range(5):
+        cross2[s, u, 0:64, :] = sides[u]
+        cross2[s, u, 64:72, :] = plain[u]
     for k in range(1, 3):
-        cross_copy(k).start()
-    mu, istd2 = moments(1, 128)
+        cross_copy(1, cross2, k).start()
+    mu2, istd2 = moments(1, 128)
+    mu = mu2
     acc3 = jnp.zeros((8, 256), f32)
     for p in range(4):
         xhat = (pre2[p] - mu) * istd2
         act, slope = gates(gain2 * xhat + shift2)
         pre2[p] = xhat
         slope2[p] = slope
+        if p == 0:
+            edge3[0] = xhat.astype(bf16)
+        if p == 3:
+            edge3[1] = xhat.astype(bf16)
         act = act.astype(bf16)
         act2[p] = act
         for q in range(2):
@@ -391,6 +440,7 @@
 
     sq = lax.fori_loop(0, 8, square, jnp.zeros((8, 256), f32))
     send_stats(2, mean, total(sq))
+    halo(edge3, halo3, 2)
     cot_copy.wait()
     gain3, shift3 = g3[...], s3[...]
     mu, istd3 = moments(2, 256)
@@ -411,6 +461,28 @@
     sd, sx = lax.fori_loop(0, 8, third, (zero8, zero8))
     sd3, sx3 = total(sd), total(sx)
     send_stats(3, sd3, sx3)
+
+    take_cross(0, cross)
+    shifts = [down2(xbuf[0, j, 0:1, 0:128] - mu1) for j in range(3)]
+    excess1[...] = cross[s] * (1.0 / local) - (cross[0] + cross[1] + cross[2]) * (1.0 / count)
+    own = down2(xbuf[0, s, 0:1, 0:128] - mu1) * cross[s, 64:65, :]
+    whole = sum(shifts[j] * cross[j, 64:65, :] for j in range(3))
+    excess1[0:64, :] = down2(istd1) * (
+        excess1[0:64, :] + own * (1.0 / local) - whole * (1.0 / count)
+    )
+    take_cross(1, cross2)
+    shifts = [down(xbuf[1, j, 0:1, 0:128] - mu2) for j in range(3)]
+    own_shift = down(xbuf[1, s, 0:1, 0:128] - mu2)
+    scale2 = down(istd2)
+    for u in range(5):
+        excess2[u] = cross2[s, u] * (1.0 / local) - (
+            cross2[0, u] + cross2[1, u] + cross2[2, u]
+        ) * (1.0 / count)
+        own = own_shift * cross2[s, u, 64:65, :]
+        whole = sum(shifts[j] * cross2[j, u, 64:65, :] for j in range(3))
+        excess2[u, 0:64, :] = scale2 * (
+            excess2[u, 0:64, :] + own * (1.0 / local) - whole * (1.0 / count)
+        )
     sd, sx = sums(3, 256)
     k0 = gain3 * istd3
     k1 = k0 * sd * (1.0 / count)
@@ -428,40 +500,17 @@
         sx_acc += part_sum(g * pre2[p])
     sd2, sx2 = both(sd_acc), both(sx_acc)
     send_stats(4, sd2, sx2)
-    act_t = act2[...].reshape(rows, 128).T
-    expand = dotf(act_t[0:64], dh3[0].reshape(rows, 256)) + dotf(
-        act_t[64:128], dh3[1].reshape(rows, 256)
-    )
-    sd, sx = sums(4, 128)
     k0 = gain2 * istd2
-    k1 = k0 * sd * (1.0 / count)
-    k2 = k0 * sx * (1.0 / count)
-    pieces = []
+    own_sd = sd2 * (1.0 / local)
+    own_sx = sx2 * (1.0 / local)
     for p in (0, 3, 1, 2):
-        dh = k0 * grad2[p] - k1 - k2 * pre2[p]
+        rest = grad2[p] - own_sd - pre2[p] * own_sx
         if p == 0:
-            edge2[0] = dh.astype(bf16)
+            edge2[0] = rest.astype(bf16)
         if p == 3:
-            edge2[1] = dh.astype(bf16)
+            edge2[1] = rest.astype(bf16)
             halo(edge2, halo2, 1)
-        widen(wide2, p + 1, dh)
-
-    sd_acc = jnp.zeros((8, 128), f32)
-    sx_acc = jnp.zeros((8, 128), f32)
-
-    def first_back(p, v, sd_acc, sx_acc):
-        g = v * slope1[p]
-        grad1[p] = g
-        return sd_acc + part_sum(g), sx_acc + part_sum(g * pre1[p])
-
-    v = conv_bwd(1, 2)
-    sd_acc, sx_acc = first_back(1, v[0:cols], sd_acc, sx_acc)
-    sd_acc, sx_acc = first_back(2, v[cols : 2 * cols], sd_acc, sx_acc)
-    take_halo(edge2, halo2, wide2, 1, lambda c, f: c)
-    for p in (0, 3):
-        sd_acc, sx_acc = first_back(p, conv_bwd(p, 1), sd_acc, sx_acc)
-    sd1, sx1 = both(sd_acc), both(sx_acc)
-    send_stats(5, sd1, sx1)
+        dh1[p] = (k0 * rest).astype(bf16)
 
     main_rows = MAIN_ROWS // ends
     late_rows = LATE_ROWS // ends
@@ -475,40 +524,53 @@
             main_a[piece, off : off + size, :] = block[done : done + size].astype(bf16)
             done += size
 
-    dh2_t = wide2[cols : cols + rows, 128:256].T
-    low = lax.broadcasted_iota(jnp.int32, (64, 128), 1) < 64
-    taps = []
-    for a in range(3):
-        g = dotf(dh2_t, wide1[a * cols : a * cols + rows, :])
-        for b in range(3):
-            g0 = g[0:64, b * 128 : (b + 1) * 128]
-            g1v = g[64:128, b * 128 : (b + 1) * 128]
-            if (3 * a + b) % 2 == 0:
-                taps.append(g0 + pltpu.roll(g1v, 64, 1))
-            else:
-                taps.append(pltpu.roll(g0, 64, 1) + g1v)
-    taps.append(jnp.zeros((64, 128), f32))
+    rest_t = dh1[...].reshape(rows, 128).T
+    taps = folded([dotf(rest_t, wide1[a * cols : a * cols + rows, :]) for a in range(3)])
+    by_sd, by_sx = down(k0 * sd2), down(k0 * sx2)
     for u in range(5):
-        put_main(64 * u, jnp.where(low, taps[2 * u], taps[2 * u + 1]))
+        put_main(64 * u, taps[u] + by_sd * excess2[u, 64:65, :] + by_sx * excess2[u, 0:64, :])
+    act_t = act2[...].reshape(rows, 128).T
+    expand = dotf(act_t[0:64], dh3[0].reshape(rows, 256)) + dotf(
+        act_t[64:128], dh3[1].reshape(rows, 256)
+    )
     put_main(320, expand[:, 0:128])
     put_main(384, expand[:, 128:256])
-    low1 = lax.broadcasted_iota(jnp.int32, (1, 128), 1) < 64
-    vec = jnp.concatenate(
-        [
-            sx3[:, 0:128], sx3[:, 128:256], sd3[:, 0:128], sd3[:, 128:256],
-            jnp.where(low1, sx2, sd2), jnp.where(low1, sx1, sd1),
-            jnp.zeros((2, 128), f32),
-        ],
-        axis=0,
-    )
-    vec_high = vec.astype(bf16)
-    vec_low = vec - vec_high.astype(f32)
-    put_main(VEC, jnp.concatenate([vec_high.astype(f32), vec_low], axis=0))
-    put_main(VEC + 16, jnp.zeros((48, 128), f32))
+    put_main(448, jnp.zeros((64, 128), f32))
     main_ra[end] = main_a[end]
 
     a_src, a_dst = (lambda t: main_a.at[t]), (lambda me: main_ra.at[me])
     spread_out(0, "a", a_src, a_dst)
+
+    sd, sx = sums(4, 128)
+    k1 = k0 * sd * (1.0 / count)
+    k2 = k0 * sx * (1.0 / count)
+    for p in range(4):
+        widen(wide2, p + 1, k0 * grad2[p] - k1 - k2 * pre2[p])
+
+    sd_acc = jnp.zeros((8, 128), f32)
+    sx_acc = jnp.zeros((8, 128), f32)
+
+    def first_back(p, v, sd_acc, sx_acc):
+        g = v * slope1[p]
+        grad1[p] = g
+        return sd_acc + part_sum(g), sx_acc + part_sum(g * pre1[p])
+
+    v = conv_bwd(1, 2)
+    sd_acc, sx_acc = first_back(1, v[0:cols], sd_acc, sx_acc)
+    sd_acc, sx_acc = first_back(2, v[cols : 2 * cols], sd_acc, sx_acc)
+    take_halo(edge3, halo3, None, 2, None)
+
+    def halo_grad(c, f):
+        xhat = halo3[0 if f is before else 1].astype(f32)
+        by_one = xbuf[4, f, 0:1, 0:128] * (1.0 / local) - sd * (1.0 / count)
+        by_xhat = xbuf[4, f, 1:2, 0:128] * (1.0 / local) - sx * (1.0 / count)
+        return k0 * (c + by_one + xhat * by_xhat)
+
+    take_halo(edge2, halo2, wide2, 1, halo_grad)
+    for p in (0, 3):
+        sd_acc, sx_acc = first_back(p, conv_bwd(p, 1), sd_acc, sx_acc)
+    sd1, sx1 = both(sd_acc), both(sx_acc)
+    send_stats(5, sd1, sx1)
 
     k0 = gain1 * istd1
     own_sd = sd1 * (1.0 / local)
@@ -519,20 +581,7 @@
     reduce = dotf(rest_t[0:64], img_v[0].reshape(rows, 256)) + dotf(
         rest_t[64:128], img_v[1].reshape(rows, 256)
     )
-    for k in range(1, 3):
-        f = lax.rem(s + k, spaces)
-        pltpu.make_async_remote_copy(
-            src_ref=cross.at[f], dst_ref=cross.at[f],
-            send_sem=cs_sem.at[k], recv_sem=cr_sem.at[f],
-            device_id=(d, f), device_id_type=MESH,
-        ).wait_recv()
-    excess = cross[s] * (1.0 / local) - (cross[0] + cross[1] + cross[2]) * (1.0 / count)
-
-    def down(row):
-        column = jnp.broadcast_to(row, (128, 128)).T[0:64]
-        return jnp.concatenate([column, column], axis=1)
-
-    reduce += down(k0 * sd1) * excess[64:65] + down(k0 * sx1) * excess[0:64]
+    reduce += down2(k0 * sd1) * excess1[64:65, :] + down2(k0 * sx1) * excess1[0:64, :]
     for h in range(2):
         for piece in range(ends):
             lo, hi = piece * late_rows, (piece + 1) * late_rows
@@ -545,6 +594,20 @@
     la_src, la_dst = (lambda t: late_a.at[t]), (lambda me: late_ra.at[me])
     spread_out(5, "a", la_src, la_dst)
 
+    low1 = lax.broadcasted_iota(jnp.int32, (1, 128), 1) < 64
+    vec_a[end] = jnp.concatenate(
+        [
+            sx3[:, 0:128], sx3[:, 128:256], sd3[:, 0:128], sd3[:, 128:256],
+            jnp.where(low1, sx2, sd2), jnp.where(low1, sx1, sd1),
+            jnp.zeros((2, 128), f32),
+        ],
+        axis=0,
+    )
+    va_src, va_dst = (lambda t: vec_a.at[end]), (lambda me: vec_a.at[me])
+    vb_src, vb_dst = (lambda t: vec_b.at[y]), (lambda me: vec_b.at[me])
+    vc_src, vc_dst = (lambda t: vec_c.at[z]), (lambda me: vec_c.at[me])
+    spread_out(9, "a", va_src, va_dst)
+
     collect(0, "a", a_src, a_dst)
     part = added(main_ra, ends)
     sub = main_rows // ys
@@ -568,6 +631,9 @@
 
     lax.fori_loop(0, 2, last, 0)
 
+    collect(9, "a", va_src, va_dst)
+    vec_b[y] = added(vec_a, ends)
+    spread_out(10, "b", vb_src, vb_dst)
     collect(5, "a", la_src, la_dst)
     late_b[y] = added(late_ra, ends).astype(bf16)
     lb_src, lb_dst = (lambda t: late_b.at[y]), (lambda me: late_b.at[me])
@@ -580,6 +646,9 @@
 
     lax.fori_loop(2, 4, last, 0)
 
+    collect(10, "b", vb_src, vb_dst)
+    vec_c[z] = added(vec_b, ys)
+    spread_out(11, "c", vc_src, vc_dst)
     collect(6, "b", lb_src, lb_dst)
     late_c[z] = added(late_b, ys).astype(bf16)
     lc_src, lc_dst = (lambda t: late_c.at[z]), (lambda me: late_c.at[me])
@@ -596,25 +665,17 @@
     spread_out(8, "a", lg_src, lg_dst)
 
     collect(3, "b", gb_src, gb_dst)
-    whole = main_gb[...].reshape(main_rows, 128)
-    main_ga[end] = whole.astype(bf16)
-
-    @pl.when(end == VEC // main_rows)
-    def _():
-        at = VEC % main_rows
-        v = whole[at : at + 8] + whole[at + 8 : at + 16]
-        v_high = v.astype(bf16).astype(f32)
-        main_ga[end, at : at + 16, :] = jnp.concatenate([v_high, v - v_high], axis=0).astype(bf16)
-
+    main_ga[end] = main_gb[...].reshape(main_rows, 128).astype(bf16)
     ga_src, ga_dst = (lambda t: main_ga.at[end]), (lambda me: main_ga.at[me])
     spread_out(4, "a", ga_src, ga_dst)
 
     scale = 1.0 / lax.axis_size("dp")
+    collect(11, "c", vc_src, vc_dst)
+    o_vec[...] = added(vec_c, zs) * scale
     collect(8, "a", lg_src, lg_dst)
     late = late_ga[...].reshape(LATE_ROWS, 128).astype(f32) * scale
     o_reduce[:, 0:128] = late[0:64]
     o_reduce[:, 128:256] = late[64:128]
-
     collect(4, "a", ga_src, ga_dst)
     main = main_ga[...].reshape(MAIN_ROWS, 128).astype(f32) * scale
     for u in range(5):
@@ -625,8 +686,6 @@
             o_dilated[2 * u + 1] = pair[64:128, 0:64]
     o_expand[:, 0:128] = main[320:384]
     o_expand[:, 128:256] = main[384:448]
-    o_vec[...] = main[VEC : VEC + 8] + main[VEC + 8 : VEC + 16]
-
     outs = []
     for k, (src, dst) in enumerate(
         ((o_reduce, h_reduce), (o_dilated, h_dilated), (o_expand, h_expand), (o_vec, h_vec))
@@ -642,13 +701,16 @@
                 device_id=(d, lax.rem(s + k, spaces)), device_id_type=MESH,
             ).wait_send()
     for k in range(1, 3):
-        cross_copy(k).wait_send()
+        cross_copy(0, cross, k).wait_send()
+        cross_copy(1, cross2, k).wait_send()
     end_halo(edge1, halo1, 0)
     end_halo(edge2, halo2, 1)
+    end_halo(edge3, halo3, 2)
     for stage, name, src, dst in (
         (0, "a", a_src, a_dst), (1, "b", b_src, b_dst), (2, "c", c_src, c_dst),
         (3, "b", gb_src, gb_dst), (4, "a", ga_src, ga_dst), (5, "a", la_src, la_dst),
         (6, "b", lb_src, lb_dst), (7, "c", lc_src, lc_dst), (8, "a", lg_src, lg_dst),
+        (9, "a", va_src, va_dst), (10, "b", vb_src, vb_dst), (11, "c", vc_src, vc_dst),
     ):
         for k in range(1, groups[name][0]):
             copy_to(stage, name, src, dst, k).wait_send()
@@ -748,10 +810,15 @@
                 pltpu.VMEM((2, 288, 128), bf16),
                 pltpu.VMEM((2, 288, 128), bf16),
                 pltpu.VMEM((2, 288, 128), bf16),
+                pltpu.VMEM((2, 288, 128), bf16),
+                pltpu.VMEM((2, 288, 128), bf16),
                 pltpu.VMEM((6 * 288, 384), bf16),
                 pltpu.VMEM((6 * 288, 384), bf16),
                 pltpu.VMEM((6, 3, 8, 256), f32),
                 pltpu.VMEM((3, 72, 256), f32),
+                pltpu.VMEM((3, 5, 72, 128), f32),
+                pltpu.VMEM((72, 256), f32),
+                pltpu.VMEM((5, 72, 128), f32),
                 pltpu.VMEM((ends, main_rows, 128), bf16),
                 pltpu.VMEM((ends, main_rows, 128), bf16),
                 pltpu.VMEM((ys, sub, 128), f32),
@@ -764,16 +831,19 @@
                 pltpu.VMEM((ys, late_rows, 128), bf16),
                 pltpu.VMEM((zs, late_rows, 128), bf16),
                 pltpu.VMEM((ends, late_rows, 128), bf16),
+                pltpu.VMEM((ends, 8, 128), f32),
+                pltpu.VMEM((ys, 8, 128), f32),
+                pltpu.VMEM((zs, 8, 128), f32),
                 pltpu.SemaphoreType.DMA((18,)),
                 pltpu.SemaphoreType.DMA((3, 8)),
-                pltpu.SemaphoreType.DMA((2, 2)),
-                pltpu.SemaphoreType.DMA((2, 2)),
+                pltpu.SemaphoreType.DMA((3, 2)),
+                pltpu.SemaphoreType.DMA((3, 2)),
                 pltpu.SemaphoreType.DMA((6, 2)),
                 pltpu.SemaphoreType.DMA((6, 3)),
-                pltpu.SemaphoreType.DMA((3,)),
-                pltpu.SemaphoreType.DMA((3,)),
-                pltpu.SemaphoreType.DMA((9, 12)),
-                pltpu.SemaphoreType.DMA((9, 12)),
+                pltpu.SemaphoreType.DMA((2, 3)),
+                pltpu.SemaphoreType.DMA((2, 3)),
+                pltpu.SemaphoreType.DMA((12, 12)),
+                pltpu.SemaphoreType.DMA((12, 12)),
             ],
             compiler_params=pltpu.CompilerParams(
                 collective_id=0, has_side_effects=True, vmem_limit_bytes=60 * 1024 * 1024

time: 79.1 us -> 78.3 us (0.990)
  Pallas kernels: 78.3 us -> 77.5 us
where the time goes in v4:
time: 78.3 us; the launch traced here: 78.2 us
  Pallas kernels  77.5 us (99%)
    pallas_call x1, Pallas kernels, shards(): pl.pallas_call(functools.partial(kernel, splits), out_shape=(big, big, ja...  74.7 us
    pallas_call x1, Pallas kernels, shards(): pl.pallas_call(store, out_shape=tuple((jax.ShapeDtypeStruct(x.shape, x.dt...  2.8 us

profile of v4, /device:TPU:1, one launch (start us, length us, event | category | flops | bytes accessed | tf_op | source)
XLA Modules:
  0.0 78.2 jit_solution(14392948248352404101)
XLA Ops:
  0.6 74.7 %shard_map.194 = (bf16[1,8,288,256]{3,2,1,0:T(8,128)(2,1)}, bf16[1,8,288,256]{3,2,1,0:T(8,128)(2,1)}, f32[64,256]{1,0:T(8,128)}, f32[9,64,64]{2,1,0:T(8,128)}, f32[64,256]{1,0:T(8,128)}, /*index=5*/f32[8,128]{1,0:T(8,128)}) custom-call(bf16[1,8,288,256]{3,2,1,0:T(8,128)(2,1)} %images.1, bf16[64,256]{1,0:T(8,128)(2,1)} %bitcast.15, ...), custom_call_target="tpu_custom_call" | custom-call | tf_op jit(solution)/shard_map/pallas_call | solution.py:772
  75.4 2.8 %shard_map.195 = (bf16[1,8,288,256]{3,2,1,0:T(8,128)(2,1)}, bf16[1,8,288,256]{3,2,1,0:T(8,128)(2,1)}, f32[64,256]{1,0:T(8,128)}, f32[9,64,64]{2,1,0:T(8,128)}, f...) custom-call(bf16[1,8,288,256]{3,2,1,0:T(8,128)(2,1)} %get-tuple-elem, ...), custom_call_target="tpu_custom_call" | custom-call | tf_op jit(solution)/shard_map/pallas_call | solution.py:856

commit v5 on v4

--- a/solution.py
+++ b/solution.py
@@ -59,7 +59,6 @@
     xbuf, cross, cross2, excess1, excess2,
     main_a, main_ra, main_b, main_rb, main_c, main_gb, main_ga,
     late_a, late_ra, late_b, late_c, late_ga,
-    vec_a, vec_b, vec_c,
     in_sem, out_sem, hs_sem, hr_sem, xs_sem, xr_sem, cs_sem, cr_sem, send_sem, recv_sem,
 ):
     ends, ys, highs = splits
@@ -120,6 +119,229 @@
     zero_out = jnp.zeros((64, 256), bf16)
     w_in[0] = jnp.concatenate([wr[...], zero_out], axis=0)
     w_in[1] = jnp.concatenate([zero_out, wr[...]], axis=0)
+    def twice(ref):
+        v = ref[...]
+        return jnp.concatenate([v, v], axis=1)
+
+    def send_stats(idx, first, second):
+        lanes = first.shape[1]
+        xbuf[idx, s, 0:1, 0:lanes] = first
+        xbuf[idx, s, 1:2, 0:lanes] = second
+        for k in range(1, 3):
+            pltpu.make_async_remote_copy(
+                src_ref=xbuf.at[idx, s],
+                dst_ref=xbuf.at[idx, s],
+                send_sem=xs_sem.at[idx, k - 1],
+                recv_sem=xr_sem.at[idx, s],
+                device_id=(d, lax.rem(s + k, spaces)),
+                device_id_type=MESH,
+            ).start()
+
+    def wait_stats(idx, lanes):
+        for k in range(1, 3):
+            f = lax.rem(s + k, spaces)
+            pltpu.make_async_remote_copy(
+                src_ref=xbuf.at[idx, f],
+                dst_ref=xbuf.at[idx, f],
+                send_sem=xs_sem.at[idx, k - 1],
+                recv_sem=xr_sem.at[idx, f],
+                device_id=(d, f),
+                device_id_type=MESH,
+            ).wait_recv()
+        firsts = [xbuf[idx, j, 0:1, 0:lanes] for j in range(3)]
+        seconds = [xbuf[idx, j, 1:2, 0:lanes] for j in range(3)]
+        return firsts, seconds
+
+    def moments(idx, lanes):
+        means, squares = wait_stats(idx, lanes)
+        mu = (means[0] + means[1] + means[2]) * (1.0 / 3.0)
+        spread = sum((m - mu) * (m - mu) for m in means)
+        var = (squares[0] + squares[1] + squares[2] + local * spread) * (1.0 / count)
+        return mu, lax.rsqrt(var + epsilon)
+
+    def sums(idx, lanes):
+        firsts, seconds = wait_stats(idx, lanes)
+        return firsts[0] + firsts[1] + firsts[2], seconds[0] + seconds[1] + seconds[2]
+
+    def halo(edge, halos, which):
+        @pl.when(s > 0)
+        def _():
+            pltpu.make_async_remote_copy(
+                src_ref=edge.at[0], dst_ref=halos.at[1],
+                send_sem=hs_sem.at[which, 0], recv_sem=hr_sem.at[which, 1],
+                device_id=(d, s - 1), device_id_type=MESH,
+            ).start()
+
+        @pl.when(s < spaces - 1)
+        def _():
+            pltpu.make_async_remote_copy(
+                src_ref=edge.at[1], dst_ref=halos.at[0],
+                send_sem=hs_sem.at[which, 1], recv_sem=hr_sem.at[which, 0],
+                device_id=(d, s + 1), device_id_type=MESH,
+            ).start()
+
+    def widen(wide, pair, x):
+        at = pair * cols
+        spot = lax.broadcasted_iota(jnp.int32, (cols, 128), 0)
+        left = jnp.where(spot >= 2, pltpu.roll(x, 2, 0), 0.0)
+        right = jnp.where(spot < cols - 2, pltpu.roll(x, cols - 2, 0), 0.0)
+        wide[at : at + cols, 0:128] = left.astype(bf16)
+        wide[at : at + cols, 128:256] = x.astype(bf16)
+        wide[at : at + cols, 256:384] = right.astype(bf16)
+
+    def take_halo(edge, halos, wide, which, finish):
+        @pl.when(s > 0)
+        def _():
+            pltpu.make_async_remote_copy(
+                src_ref=edge.at[1], dst_ref=halos.at[0],
+                send_sem=hs_sem.at[which, 0], recv_sem=hr_sem.at[which, 0],
+                device_id=(d, s - 1), device_id_type=MESH,
+            ).wait_recv()
+            if wide is not None:
+                widen(wide, 0, finish(halos[0].astype(f32), before))
+
+        @pl.when(s < spaces - 1)
+        def _():
+            pltpu.make_async_remote_copy(
+                src_ref=edge.at[0], dst_ref=halos.at[1],
+                send_sem=hs_sem.at[which, 1], recv_sem=hr_sem.at[which, 1],
+                device_id=(d, s + 1), device_id_type=MESH,
+            ).wait_recv()
+            if wide is not None:
+                widen(wide, 5, finish(halos[1].astype(f32), after))
+
+    def end_halo(edge, halos, which):
+        @pl.when(s > 0)
+        def _():
+            pltpu.make_async_remote_copy(
+                src_ref=edge.at[0], dst_ref=halos.at[1],
+                send_sem=hs_sem.at[which, 0], recv_sem=hr_sem.at[which, 1],
+                device_id=(d, s - 1), device_id_type=MESH,
+            ).wait_send()
+
+        @pl.when(s < spaces - 1)
+        def _():
+            pltpu.make_async_remote_copy(
+                src_ref=edge.at[1], dst_ref=halos.at[0],
+                send_sem=hs_sem.at[which, 1], recv_sem=hr_sem.at[which, 0],
+                device_id=(d, s + 1), device_id_type=MESH,
+            ).wait_send()
+
+    def conv_fwd(pair, n):
+        acc = dotf(wide1[pair * cols : (pair + n) * cols, :], w_fwd[0])
+        for a in range(1, 3):
+            acc += dotf(wide1[(pair + a) * cols : (pair + a + n) * cols, :], w_fwd[a])
+        return acc
+
+    def conv_bwd(pair, n):
+        acc = dot_t(wide2[pair * cols : (pair + n) * cols, :], w_bwd[0])
+        for a in range(1, 3):
+            acc += dot_t(wide2[(pair + a) * cols : (pair + a + n) * cols, :], w_bwd[a])
+        return acc
+
+    def local_moments(idx, pre, acc, early=None):
+        mean = both(acc) * (1.0 / local)
+        if early is not None:
+            early(mean)
+        sq = jnp.zeros((8, 128), f32)
+        for p in range(4):
+            c = pre[p] - mean
+            sq += part_sum(c * c)
+        send_stats(idx, mean, both(sq))
+        return mean
+
+    def high_low(x):
+        high = x.astype(bf16)
+        low = (x - high.astype(f32)).astype(bf16)
+        return high.T, low.T
+
+    def folded(g):
+        taps = []
+        for t in range(9):
+            a, b = divmod(t, 3)
+            block = g[a][:, b * 128 : (b + 1) * 128]
+            n = block.shape[0] // 2 if block.shape[0] > 8 else 8
+            even, odd = block[0:n], block[block.shape[0] - n :]
+            if t % 2 == 0:
+                taps.append(even + pltpu.roll(odd, 64, 1))
+            else:
+                taps.append(pltpu.roll(even, 64, 1) + odd)
+        taps.append(jnp.zeros_like(taps[0]))
+        low = lax.broadcasted_iota(jnp.int32, taps[0].shape, 1) < 64
+        return [jnp.where(low, taps[2 * u], taps[2 * u + 1]) for u in range(5)]
+
+    def down(row):
+        return jnp.broadcast_to(row, (128, 128)).T[0:64]
+
+    def down2(row):
+        return jnp.concatenate([down(row)] * 2, axis=1)
+
+    def cross_copy(which, buf, k):
+        return pltpu.make_async_remote_copy(
+            src_ref=buf.at[s], dst_ref=buf.at[s],
+            send_sem=cs_sem.at[which, k], recv_sem=cr_sem.at[which, s],
+            device_id=(d, lax.rem(s + k, spaces)), device_id_type=MESH,
+        )
+
+    def take_cross(which, buf):
+        for k in range(1, 3):
+            f = lax.rem(s + k, spaces)
+            pltpu.make_async_remote_copy(
+                src_ref=buf.at[f], dst_ref=buf.at[f],
+                send_sem=cs_sem.at[which, k], recv_sem=cr_sem.at[which, f],
+                device_id=(d, f), device_id_type=MESH,
+            ).wait_recv()
+
+    rows = 4 * cols
+    ones = jnp.ones((16, rows), bf16)
+
+    def copy_to(stage, name, src, dst, k):
+        n, me, ident = groups[name]
+        t = lax.rem(me + k, n)
+        return pltpu.make_async_remote_copy(
+            src_ref=src(t), dst_ref=dst(me),
+            send_sem=send_sem.at[stage, k], recv_sem=recv_sem.at[stage, me],
+            device_id=ident(t), device_id_type=MESH,
+        )
+
+    def spread_out(stage, name, src, dst):
+        for k in range(1, groups[name][0]):
+            copy_to(stage, name, src, dst, k).start()
+
+    def collect(stage, name, src, dst):
+        n, me, ident = groups[name]
+        for k in range(1, n):
+            f = lax.rem(me + k, n)
+            pltpu.make_async_remote_copy(
+                src_ref=src(f), dst_ref=dst(f),
+                send_sem=send_sem.at[stage, k], recv_sem=recv_sem.at[stage, f],
+                device_id=ident(f), device_id_type=MESH,
+            ).wait_recv()
+
+    def added(ref, n):
+        acc = ref[0].astype(f32)
+        for k in range(1, n):
+            acc += ref[k].astype(f32)
+        return acc
+
+    acc = jnp.zeros((8, 128), f32)
+    for p in range(4):
+        in_copies[2 * p].wait()
+        in_copies[2 * p + 1].wait()
+        v = dot_t(img_v[0, p], w_in[0]) + dot_t(img_v[1, p], w_in[1])
+        pre1[p] = v
+        acc += part_sum(v)
+    gain1, shift1 = twice(g1), twice(s1)
+    gain2, shift2 = twice(g2), twice(s2)
+    pl.semaphore_wait(barrier, partners)
+
+    def early(mean):
+        edge1[0] = (pre1[0] - mean).astype(bf16)
+        edge1[1] = (pre1[3] - mean).astype(bf16)
+        halo(edge1, halo1, 0)
+
+    mean1 = local_moments(0, pre1, acc, early)
+
     w_out[0] = jnp.concatenate([we[...], zero_out], axis=0)
     w_out[1] = jnp.concatenate([zero_out, we[...]], axis=0)
     zero_mid = jnp.zeros((64, 64), bf16)
@@ -145,229 +367,6 @@
     def _():
         wide1[5 * cols : 6 * cols, :] = jnp.zeros((cols, 384), bf16)
         wide2[5 * cols : 6 * cols, :] = jnp.zeros((cols, 384), bf16)
-
-    def twice(ref):
-        v = ref[...]
-        return jnp.concatenate([v, v], axis=1)
-
-    def send_stats(idx, first, second):
-        lanes = first.shape[1]
-        xbuf[idx, s, 0:1, 0:lanes] = first
-        xbuf[idx, s, 1:2, 0:lanes] = second
-        for k in range(1, 3):
-            pltpu.make_async_remote_copy(
-                src_ref=xbuf.at[idx, s],
-                dst_ref=xbuf.at[idx, s],
-                send_sem=xs_sem.at[idx, k - 1],
-                recv_sem=xr_sem.at[idx, s],
-                device_id=(d, lax.rem(s + k, spaces)),
-                device_id_type=MESH,
-            ).start()
-
-    def wait_stats(idx, lanes):
-        for k in range(1, 3):
-            f = lax.rem(s + k, spaces)
-            pltpu.make_async_remote_copy(
-                src_ref=xbuf.at[idx, f],
-                dst_ref=xbuf.at[idx, f],
-                send_sem=xs_sem.at[idx, k - 1],
-                recv_sem=xr_sem.at[idx, f],
-                device_id=(d, f),
-                device_id_type=MESH,
-            ).wait_recv()
-        firsts = [xbuf[idx, j, 0:1, 0:lanes] for j in range(3)]
-        seconds = [xbuf[idx, j, 1:2, 0:lanes] for j in range(3)]
-        return firsts, seconds
-
-    def moments(idx, lanes):
-        means, squares = wait_stats(idx, lanes)
-        mu = (means[0] + means[1] + means[2]) * (1.0 / 3.0)
-        spread = sum((m - mu) * (m - mu) for m in means)
-        var = (squares[0] + squares[1] + squares[2] + local * spread) * (1.0 / count)
-        return mu, lax.rsqrt(var + epsilon)
-
-    def sums(idx, lanes):
-        firsts, seconds = wait_stats(idx, lanes)
-        return firsts[0] + firsts[1] + firsts[2], seconds[0] + seconds[1] + seconds[2]
-
-    def halo(edge, halos, which):
-        @pl.when(s > 0)
-        def _():
-            pltpu.make_async_remote_copy(
-                src_ref=edge.at[0], dst_ref=halos.at[1],
-                send_sem=hs_sem.at[which, 0], recv_sem=hr_sem.at[which, 1],
-                device_id=(d, s - 1), device_id_type=MESH,
-            ).start()
-
-        @pl.when(s < spaces - 1)
-        def _():
-            pltpu.make_async_remote_copy(
-                src_ref=edge.at[1], dst_ref=halos.at[0],
-                send_sem=hs_sem.at[which, 1], recv_sem=hr_sem.at[which, 0],
-                device_id=(d, s + 1), device_id_type=MESH,
-            ).start()
-
-    def widen(wide, pair, x):
-        at = pair * cols
-        spot = lax.broadcasted_iota(jnp.int32, (cols, 128), 0)
-        left = jnp.where(spot >= 2, pltpu.roll(x, 2, 0), 0.0)
-        right = jnp.where(spot < cols - 2, pltpu.roll(x, cols - 2, 0), 0.0)
-        wide[at : at + cols, 0:128] = left.astype(bf16)
-        wide[at : at + cols, 128:256] = x.astype(bf16)
-        wide[at : at + cols, 256:384] = right.astype(bf16)
-
-    def take_halo(edge, halos, wide, which, finish):
-        @pl.when(s > 0)
-        def _():
-            pltpu.make_async_remote_copy(
-                src_ref=edge.at[1], dst_ref=halos.at[0],
-                send_sem=hs_sem.at[which, 0], recv_sem=hr_sem.at[which, 0],
-                device_id=(d, s - 1), device_id_type=MESH,
-            ).wait_recv()
-            if wide is not None:
-                widen(wide, 0, finish(halos[0].astype(f32), before))
-
-        @pl.when(s < spaces - 1)
-        def _():
-            pltpu.make_async_remote_copy(
-                src_ref=edge.at[0], dst_ref=halos.at[1],
-                send_sem=hs_sem.at[which, 1], recv_sem=hr_sem.at[which, 1],
-                device_id=(d, s + 1), device_id_type=MESH,
-            ).wait_recv()
-            if wide is not None:
-                widen(wide, 5, finish(halos[1].astype(f32), after))
-
-    def end_halo(edge, halos, which):
-        @pl.when(s > 0)
-        def _():
-            pltpu.make_async_remote_copy(
-                src_ref=edge.at[0], dst_ref=halos.at[1],
-                send_sem=hs_sem.at[which, 0], recv_sem=hr_sem.at[which, 1],
-                device_id=(d, s - 1), device_id_type=MESH,
-            ).wait_send()
-
-        @pl.when(s < spaces - 1)
-        def _():
-            pltpu.make_async_remote_copy(
-                src_ref=edge.at[1], dst_ref=halos.at[0],
-                send_sem=hs_sem.at[which, 1], recv_sem=hr_sem.at[which, 0],
-                device_id=(d, s + 1), device_id_type=MESH,
-            ).wait_send()
-
-    def conv_fwd(pair, n):
-        acc = dotf(wide1[pair * cols : (pair + n) * cols, :], w_fwd[0])
-        for a in range(1, 3):
-            acc += dotf(wide1[(pair + a) * cols : (pair + a + n) * cols, :], w_fwd[a])
-        return acc
-
-    def conv_bwd(pair, n):
-        acc = dot_t(wide2[pair * cols : (pair + n) * cols, :], w_bwd[0])
-        for a in range(1, 3):
-            acc += dot_t(wide2[(pair + a) * cols : (pair + a + n) * cols, :], w_bwd[a])
-        return acc
-
-    def local_moments(idx, pre, acc, early=None):
-        mean = both(acc) * (1.0 / local)
-        if early is not None:
-            early(mean)
-        sq = jnp.zeros((8, 128), f32)
-        for p in range(4):
-            c = pre[p] - mean
-            sq += part_sum(c * c)
-        send_stats(idx, mean, both(sq))
-        return mean
-
-    def high_low(x):
-        high = x.astype(bf16)
-        low = (x - high.astype(f32)).astype(bf16)
-        return high.T, low.T
-
-    def folded(g):
-        taps = []
-        for t in range(9):
-            a, b = divmod(t, 3)
-            block = g[a][:, b * 128 : (b + 1) * 128]
-            n = block.shape[0] // 2 if block.shape[0] > 8 else 8
-            even, odd = block[0:n], block[block.shape[0] - n :]
-            if t % 2 == 0:
-                taps.append(even + pltpu.roll(odd, 64, 1))
-            else:
-                taps.append(pltpu.roll(even, 64, 1) + odd)
-        taps.append(jnp.zeros_like(taps[0]))
-        low = lax.broadcasted_iota(jnp.int32, taps[0].shape, 1) < 64
-        return [jnp.where(low, taps[2 * u], taps[2 * u + 1]) for u in range(5)]
-
-    def down(row):
-        return jnp.broadcast_to(row, (128, 128)).T[0:64]
-
-    def down2(row):
-        return jnp.concatenate([down(row)] * 2, axis=1)
-
-    def cross_copy(which, buf, k):
-        return pltpu.make_async_remote_copy(
-            src_ref=buf.at[s], dst_ref=buf.at[s],
-            send_sem=cs_sem.at[which, k], recv_sem=cr_sem.at[which, s],
-            device_id=(d, lax.rem(s + k, spaces)), device_id_type=MESH,
-        )
-
-    def take_cross(which, buf):
-        for k in range(1, 3):
-            f = lax.rem(s + k, spaces)
-            pltpu.make_async_remote_copy(
-                src_ref=buf.at[f], dst_ref=buf.at[f],
-                send_sem=cs_sem.at[which, k], recv_sem=cr_sem.at[which, f],
-                device_id=(d, f), device_id_type=MESH,
-            ).wait_recv()
-
-    rows = 4 * cols
-    ones = jnp.ones((16, rows), bf16)
-
-    def copy_to(stage, name, src, dst, k):
-        n, me, ident = groups[name]
-        t = lax.rem(me + k, n)
-        return pltpu.make_async_remote_copy(
-            src_ref=src(t), dst_ref=dst(me),
-            send_sem=send_sem.at[stage, k], recv_sem=recv_sem.at[stage, me],
-            device_id=ident(t), device_id_type=MESH,
-        )
-
-    def spread_out(stage, name, src, dst):
-        for k in range(1, groups[name][0]):
-            copy_to(stage, name, src, dst, k).start()
-
-    def collect(stage, name, src, dst):
-        n, me, ident = groups[name]
-        for k in range(1, n):
-            f = lax.rem(me + k, n)
-            pltpu.make_async_remote_copy(
-                src_ref=src(f), dst_ref=dst(f),
-                send_sem=send_sem.at[stage, k], recv_sem=recv_sem.at[stage, f],
-                device_id=ident(f), device_id_type=MESH,
-            ).wait_recv()
-
-    def added(ref, n):
-        acc = ref[0].astype(f32)
-        for k in range(1, n):
-            acc += ref[k].astype(f32)
-        return acc
-
-    acc = jnp.zeros((8, 128), f32)
-    for p in range(4):
-        in_copies[2 * p].wait()
-        in_copies[2 * p + 1].wait()
-        v = dot_t(img_v[0, p], w_in[0]) + dot_t(img_v[1, p], w_in[1])
-        pre1[p] = v
-        acc += part_sum(v)
-    gain1, shift1 = twice(g1), twice(s1)
-    gain2, shift2 = twice(g2), twice(s2)
-    pl.semaphore_wait(barrier, partners)
-
-    def early(mean):
-        edge1[0] = (pre1[0] - mean).astype(bf16)
-        edge1[1] = (pre1[3] - mean).astype(bf16)
-        halo(edge1, halo1, 0)
-
-    mean1 = local_moments(0, pre1, acc, early)
 
     high, low = high_low(pre1[...].reshape(rows, 128) - mean1)
     crossed = jnp.zeros((144, 256), f32)
@@ -411,8 +410,6 @@
     for u in range(5):
         cross2[s, u, 0:64, :] = sides[u]
         cross2[s, u, 64:72, :] = plain[u]
-    for k in range(1, 3):
-        cross_copy(1, cross2, k).start()
     mu2, istd2 = moments(1, 128)
     mu = mu2
     acc3 = jnp.zeros((8, 256), f32)
@@ -441,6 +438,8 @@
     sq = lax.fori_loop(0, 8, square, jnp.zeros((8, 256), f32))
     send_stats(2, mean, total(sq))
     halo(edge3, halo3, 2)
+    for k in range(1, 3):
+        cross_copy(1, cross2, k).start()
     cot_copy.wait()
     gain3, shift3 = g3[...], s3[...]
     mu, istd3 = moments(2, 256)
@@ -590,12 +589,8 @@
                 late_a[piece, a - lo : b - lo, :] = reduce[
                     a - 64 * h : b - 64 * h, 128 * h : 128 * h + 128
                 ].astype(bf16)
-    late_ra[end] = late_a[end]
-    la_src, la_dst = (lambda t: late_a.at[t]), (lambda me: late_ra.at[me])
-    spread_out(5, "a", la_src, la_dst)
-
     low1 = lax.broadcasted_iota(jnp.int32, (1, 128), 1) < 64
-    vec_a[end] = jnp.concatenate(
+    vec = jnp.concatenate(
         [
             sx3[:, 0:128], sx3[:, 128:256], sd3[:, 0:128], sd3[:, 128:256],
             jnp.where(low1, sx2, sd2), jnp.where(low1, sx1, sd1),
@@ -603,10 +598,23 @@
         ],
         axis=0,
     )
-    va_src, va_dst = (lambda t: vec_a.at[end]), (lambda me: vec_a.at[me])
-    vb_src, vb_dst = (lambda t: vec_b.at[y]), (lambda me: vec_b.at[me])
-    vc_src, vc_dst = (lambda t: vec_c.at[z]), (lambda me: vec_c.at[me])
-    spread_out(9, "a", va_src, va_dst)
+
+    def parts(v):
+        v_high = v.astype(bf16).astype(f32)
+        return jnp.concatenate([v_high, v - v_high], axis=0).astype(bf16)
+
+    def packed(v):
+        at = late_rows
+        return jnp.concatenate(
+            [v[0:at].astype(bf16), parts(v[at : at + 8] + v[at + 8 : at + 16])], axis=0
+        )
+
+    vec = parts(vec)
+    for piece in range(ends):
+        late_a[piece, late_rows : late_rows + 16, :] = vec
+    late_ra[end] = late_a[end]
+    la_src, la_dst = (lambda t: late_a.at[t]), (lambda me: late_ra.at[me])
+    spread_out(5, "a", la_src, la_dst)
 
     collect(0, "a", a_src, a_dst)
     part = added(main_ra, ends)
@@ -631,11 +639,8 @@
 
     lax.fori_loop(0, 2, last, 0)
 
-    collect(9, "a", va_src, va_dst)
-    vec_b[y] = added(vec_a, ends)
-    spread_out(10, "b", vb_src, vb_dst)
     collect(5, "a", la_src, la_dst)
-    late_b[y] = added(late_ra, ends).astype(bf16)
+    late_b[y] = packed(added(late_ra, ends))
     lb_src, lb_dst = (lambda t: late_b.at[y]), (lambda me: late_b.at[me])
     spread_out(6, "b", lb_src, lb_dst)
 
@@ -646,11 +651,8 @@
 
     lax.fori_loop(2, 4, last, 0)
 
-    collect(10, "b", vb_src, vb_dst)
-    vec_c[z] = added(vec_b, ys)
-    spread_out(11, "c", vc_src, vc_dst)
     collect(6, "b", lb_src, lb_dst)
-    late_c[z] = added(late_b, ys).astype(bf16)
+    late_c[z] = packed(added(late_b, ys))
     lc_src, lc_dst = (lambda t: late_c.at[z]), (lambda me: late_c.at[me])
     spread_out(7, "c", lc_src, lc_dst)
 
@@ -660,7 +662,8 @@
     spread_out(3, "b", gb_src, gb_dst)
 
     collect(7, "c", lc_src, lc_dst)
-    late_ga[end] = added(late_c, zs).astype(bf16)
+    whole = added(late_c, zs)
+    late_ga[end] = whole[0:late_rows].astype(bf16)
     lg_src, lg_dst = (lambda t: late_ga.at[end]), (lambda me: late_ga.at[me])
     spread_out(8, "a", lg_src, lg_dst)
 
@@ -669,9 +672,33 @@
     ga_src, ga_dst = (lambda t: main_ga.at[end]), (lambda me: main_ga.at[me])
     spread_out(4, "a", ga_src, ga_dst)
 
+    def sent(*stages):
+        for stage, name, src, dst in stages:
+            for k in range(1, groups[name][0]):
+                copy_to(stage, name, src, dst, k).wait_send()
+
+    for idx in range(6):
+        for k in range(1, 3):
+            pltpu.make_async_remote_copy(
+                src_ref=xbuf.at[idx, s], dst_ref=xbuf.at[idx, s],
+                send_sem=xs_sem.at[idx, k - 1], recv_sem=xr_sem.at[idx, s],
+                device_id=(d, lax.rem(s + k, spaces)), device_id_type=MESH,
+            ).wait_send()
+    for k in range(1, 3):
+        cross_copy(0, cross, k).wait_send()
+        cross_copy(1, cross2, k).wait_send()
+    end_halo(edge1, halo1, 0)
+    end_halo(edge2, halo2, 1)
+    end_halo(edge3, halo3, 2)
+    sent(
+        (0, "a", a_src, a_dst), (1, "b", b_src, b_dst), (2, "c", c_src, c_dst), (3, "b", gb_src, gb_dst),
+        (5, "a", la_src, la_dst), (6, "b", lb_src, lb_dst), (7, "c", lc_src, lc_dst),
+    )
+    for r in range(8):
+        pltpu.make_async_copy(res_v.at[r], result.at[0, r], out_sem.at[0, r]).wait()
+        pltpu.make_async_copy(gi_v.at[r], gimages.at[0, r], out_sem.at[1, r]).wait()
     scale = 1.0 / lax.axis_size("dp")
-    collect(11, "c", vc_src, vc_dst)
-    o_vec[...] = added(vec_c, zs) * scale
+    o_vec[...] = (whole[late_rows : late_rows + 8] + whole[late_rows + 8 : late_rows + 16]) * scale
     collect(8, "a", lg_src, lg_dst)
     late = late_ga[...].reshape(LATE_ROWS, 128).astype(f32) * scale
     o_reduce[:, 0:128] = late[0:64]
@@ -693,30 +720,7 @@
         outs.append(pltpu.make_async_copy(src, dst, out_sem.at[2, k]))
         outs[-1].start()
 
-    for idx in range(6):
-        for k in range(1, 3):
-            pltpu.make_async_remote_copy(
-                src_ref=xbuf.at[idx, s], dst_ref=xbuf.at[idx, s],
-                send_sem=xs_sem.at[idx, k - 1], recv_sem=xr_sem.at[idx, s],
-                device_id=(d, lax.rem(s + k, spaces)), device_id_type=MESH,
-            ).wait_send()
-    for k in range(1, 3):
-        cross_copy(0, cross, k).wait_send()
-        cross_copy(1, cross2, k).wait_send()
-    end_halo(edge1, halo1, 0)
-    end_halo(edge2, halo2, 1)
-    end_halo(edge3, halo3, 2)
-    for stage, name, src, dst in (
-        (0, "a", a_src, a_dst), (1, "b", b_src, b_dst), (2, "c", c_src, c_dst),
-        (3, "b", gb_src, gb_dst), (4, "a", ga_src, ga_dst), (5, "a", la_src, la_dst),
-        (6, "b", lb_src, lb_dst), (7, "c", lc_src, lc_dst), (8, "a", lg_src, lg_dst),
-        (9, "a", va_src, va_dst), (10, "b", vb_src, vb_dst), (11, "c", vc_src, vc_dst),
-    ):
-        for k in range(1, groups[name][0]):
-            copy_to(stage, name, src, dst, k).wait_send()
-    for r in range(8):
-        pltpu.make_async_copy(res_v.at[r], result.at[0, r], out_sem.at[0, r]).wait()
-        pltpu.make_async_copy(gi_v.at[r], gimages.at[0, r], out_sem.at[1, r]).wait()
+    sent((4, "a", ga_src, ga_dst), (8, "a", lg_src, lg_dst))
     for c in outs:
         c.wait()
 
@@ -826,14 +830,11 @@
                 pltpu.VMEM((zs, sub, 128), f32),
                 pltpu.VMEM((ys, sub, 128), f32),
                 pltpu.VMEM((ends, main_rows, 128), bf16),
+                pltpu.VMEM((ends, late_rows + 16, 128), bf16),
+                pltpu.VMEM((ends, late_rows + 16, 128), bf16),
+                pltpu.VMEM((ys, late_rows + 16, 128), bf16),
+                pltpu.VMEM((zs, late_rows + 16, 128), bf16),
                 pltpu.VMEM((ends, late_rows, 128), bf16),
-                pltpu.VMEM((ends, late_rows, 128), bf16),
-                pltpu.VMEM((ys, late_rows, 128), bf16),
-                pltpu.VMEM((zs, late_rows, 128), bf16),
-                pltpu.VMEM((ends, late_rows, 128), bf16),
-                pltpu.VMEM((ends, 8, 128), f32),
-                pltpu.VMEM((ys, 8, 128), f32),
-                pltpu.VMEM((zs, 8, 128), f32),
                 pltpu.SemaphoreType.DMA((18,)),
                 pltpu.SemaphoreType.DMA((3, 8)),
                 pltpu.SemaphoreType.DMA((3, 2)),
@@ -842,8 +843,8 @@
                 pltpu.SemaphoreType.DMA((6, 3)),
                 pltpu.SemaphoreType.DMA((2, 3)),
                 pltpu.SemaphoreType.DMA((2, 3)),
-                pltpu.SemaphoreType.DMA((12, 12)),
-                pltpu.SemaphoreType.DMA((12, 12)),
+                pltpu.SemaphoreType.DMA((9, 12)),
+                pltpu.SemaphoreType.DMA((9, 12)),
             ],
             compiler_params=pltpu.CompilerParams(
                 collective_id=0, has_side_effects=True, vmem_limit_bytes=60 * 1024 * 1024

time: 78.3 us -> 76.2 us (0.973)
  Pallas kernels: 77.5 us -> 75.4 us
    pallas_call x1, Pallas kernels: 74.7 us -> 72.6 us  [shards(): pl.pallas_call(functools.partial(kernel, splits), out_shape=(big, big, ja...]
where the time goes in v5:
time: 76.2 us; the launch traced here: 76 us
  Pallas kernels  75.4 us (99%)
    pallas_call x1, Pallas kernels, shards(): pl.pallas_call(functools.partial(kernel, splits), out_shape=(big, big, ja...  72.6 us
    pallas_call x1, Pallas kernels, shards(): pl.pallas_call(store, out_shape=tuple((jax.ShapeDtypeStruct(x.shape, x.dt...  2.8 us

profile of v5, /device:TPU:1, one launch (start us, length us, event | category | flops | bytes accessed | tf_op | source)
XLA Modules:
  0.0 76.0 jit_solution(8401052466119256677)
XLA Ops:
  0.6 72.6 %shard_map.194 = (bf16[1,8,288,256]{3,2,1,0:T(8,128)(2,1)}, bf16[1,8,288,256]{3,2,1,0:T(8,128)(2,1)}, f32[64,256]{1,0:T(8,128)}, f32[9,64,64]{2,1,0:T(8,128)}, f32[64,256]{1,0:T(8,128)}, /*index=5*/f32[8,128]{1,0:T(8,128)}) custom-call(bf16[1,8,288,256]{3,2,1,0:T(8,128)(2,1)} %images.1, bf16[64,256]{1,0:T(8,128)(2,1)} %bitcast.15, ...), custom_call_target="tpu_custom_call" | custom-call | tf_op jit(solution)/shard_map/pallas_call | solution.py:776
  73.2 2.8 %shard_map.195 = (bf16[1,8,288,256]{3,2,1,0:T(8,128)(2,1)}, bf16[1,8,288,256]{3,2,1,0:T(8,128)(2,1)}, f32[64,256]{1,0:T(8,128)}, f32[9,64,64]{2,1,0:T(8,128)}, f...) custom-call(bf16[1,8,288,256]{3,2,1,0:T(8,128)(2,1)} %get-tuple-elem, ...), custom_call_target="tpu_custom_call" | custom-call | tf_op jit(solution)/shard_map/pallas_call | solution.py:857

commit v6 on v5

--- a/solution.py
+++ b/solution.py
@@ -87,6 +87,16 @@
 
     groups = {"a": (ends, end, id_a), "b": (ys, y, id_b), "c": (zs, z, id_c)}
 
+    barrier = pltpu.get_barrier_semaphore()
+    partners = 0
+    for name in "cba":
+        n, me, ident = groups[name]
+        for k in sorted(range(1, n), key=lambda k: -min(k, n - k)):
+            pl.semaphore_signal(
+                barrier, inc=1, device_id=ident(lax.rem(me + k, n)), device_id_type=MESH
+            )
+            partners += 1
+
     in_copies = []
     for r in range(8):
         c = pltpu.make_async_copy(images.at[0, r], img_v.at[r % 2, r // 2], in_sem.at[r])
@@ -104,16 +114,6 @@
     cot_copy = pltpu.make_async_copy(cot.at[0], cot_v, in_sem.at[8])
     cot_copy.start()
 
-    barrier = pltpu.get_barrier_semaphore()
-    partners = 0
-    for name in "cba":
-        n, me, ident = groups[name]
-        for k in sorted(range(1, n), key=lambda k: -min(k, n - k)):
-            pl.semaphore_signal(
-                barrier, inc=1, device_id=ident(lax.rem(me + k, n)), device_id_type=MESH
-            )
-            partners += 1
-
     for c in small:
         c.wait()
     zero_out = jnp.zeros((64, 256), bf16)
@@ -305,7 +305,8 @@
         )
 
     def spread_out(stage, name, src, dst):
-        for k in range(1, groups[name][0]):
+        n = groups[name][0]
+        for k in sorted(range(1, n), key=lambda k: -min(k, n - k)):
             copy_to(stage, name, src, dst, k).start()
 
     def collect(stage, name, src, dst):
@@ -435,7 +436,7 @@
         c = x3[r] - mean
         return acc + part_sum(c * c)
 
-    sq = lax.fori_loop(0, 8, square, jnp.zeros((8, 256), f32))
+    sq = lax.fori_loop(0, 8, square, jnp.zeros((8, 256), f32), unroll=4)
     send_stats(2, mean, total(sq))
     halo(edge3, halo3, 2)
     for k in range(1, 3):
@@ -705,12 +706,11 @@
     o_reduce[:, 128:256] = late[64:128]
     collect(4, "a", ga_src, ga_dst)
     main = main_ga[...].reshape(MAIN_ROWS, 128).astype(f32) * scale
-    for u in range(5):
-        pair = main[64 * u : 64 * u + 64]
-        pair = jnp.concatenate([pair, pair], axis=0).T
-        o_dilated[2 * u] = pair[0:64, 0:64]
-        if u < 4:
-            o_dilated[2 * u + 1] = pair[64:128, 0:64]
+    for u in range(3):
+        pair = main[128 * u : 128 * u + 128].T
+        for t in range(4 if u < 2 else 1):
+            a, b = 64 * (t % 2), 64 * (t // 2)
+            o_dilated[4 * u + t] = pair[a : a + 64, b : b + 64]
     o_expand[:, 0:128] = main[320:384]
     o_expand[:, 128:256] = main[384:448]
     outs = []

time: 76.2 us -> 74.8 us (0.982)
  Pallas kernels: 75.4 us -> 74 us
    pallas_call x1, Pallas kernels: 72.6 us -> 71.2 us  [shards(): pl.pallas_call(functools.partial(kernel, splits), out_shape=(big, big, ja...]
where the time goes in v6:
time: 74.8 us; the launch traced here: 74.6 us
  Pallas kernels  74 us (99%)
    pallas_call x1, Pallas kernels, shards(): pl.pallas_call(functools.partial(kernel, splits), out_shape=(big, big, ja...  71.2 us
    pallas_call x1, Pallas kernels, shards(): pl.pallas_call(store, out_shape=tuple((jax.ShapeDtypeStruct(x.shape, x.dt...  2.8 us

profile of v6, /device:TPU:1, one launch (start us, length us, event | category | flops | bytes accessed | tf_op | source)
XLA Modules:
  0.0 74.6 jit_solution(6986379421452061719)
XLA Ops:
  0.6 71.2 %shard_map.194 = (bf16[1,8,288,256]{3,2,1,0:T(8,128)(2,1)}, bf16[1,8,288,256]{3,2,1,0:T(8,128)(2,1)}, f32[64,256]{1,0:T(8,128)}, f32[9,64,64]{2,1,0:T(8,128)}, f32[64,256]{1,0:T(8,128)}, /*index=5*/f32[8,128]{1,0:T(8,128)}) custom-call(bf16[1,8,288,256]{3,2,1,0:T(8,128)(2,1)} %images.1, bf16[64,256]{1,0:T(8,128)(2,1)} %bitcast.15, ...), custom_call_target="tpu_custom_call" | custom-call | tf_op jit(solution)/shard_map/pallas_call | solution.py:776
  71.8 2.8 %shard_map.195 = (bf16[1,8,288,256]{3,2,1,0:T(8,128)(2,1)}, bf16[1,8,288,256]{3,2,1,0:T(8,128)(2,1)}, f32[64,256]{1,0:T(8,128)}, f32[9,64,64]{2,1,0:T(8,128)}, f...) custom-call(bf16[1,8,288,256]{3,2,1,0:T(8,128)(2,1)} %get-tuple-elem, ...), custom_call_target="tpu_custom_call" | custom-call | tf_op jit(solution)/shard_map/pallas_call | solution.py:857
